TPU v7x, 768 devices: a whole 4x8x12 slice. The times are simulated.
768 devices in a mesh: dp: 16 (over y, core), seq: 4 (over x), pool: 12 (over z).
Axes of the slice: x: 4, y: 8, z: 12, core: 2. Of those that a mesh axis runs over, the one named last changes fastest.
Arguments:
- events: bfloat16 [98304, 1024], P(('dp', 'seq', 'pool')), may hold values from -6 to 6
- input_weight: bfloat16 [1024, 4096], replicated, may hold values from -0.1875 to 0.1875
- output_weight: bfloat16 [1024, 1024], replicated, may hold values from -0.1875 to 0.1875
- positives: bfloat16 [98304, 1024], P(('dp', 'seq', 'pool')), may hold values from -8 to 8
- negatives: bfloat16 [1536, 1024], P('pool'), may hold values from -6 to 6
- log_probs: bfloat16 [1536], P('pool'), may hold values from -15 to -4
- lengths: int32 [768], replicated, may hold values from 1 to 256, 98304 in all
Outputs:
- d_events: float32 [98304, 1024], P(('dp', 'seq', 'pool'))
- d_output_weight: float32 [1024, 1024], P(('dp', 'seq'))
Inputs may be any that keep to these rules, and one draw needn't show every extreme that they name: The histories lie end to end over all 98304 events, their lengths sum to 98304, and one history has exactly 256 events.
All inputs are finite; a program needn't handle non-finite values.
Results may differ from a plain program's by a relative error of at most 0.0095.
Values may be sent and summed in bfloat16 or wider, within the bound.
A program may use at most 64 MiB of HBM per device.

v0:
```python
import math

import jax
import jax.numpy as jnp
from jax import lax
from jax.sharding import PartitionSpec as P

HEADS = 8
EV_DEV = 128
REACH = 2


epsilon = 1e-05
sharpness_divisor = 0.05
loss_multiplier = 8.0


def shifted(x, axis, by):
    length = lax.axis_size(axis)
    pairs = [(i, i + by) for i in range(length) if 0 <= i + by < length]
    return lax.ppermute(x, axis, pairs)


def normalize(row_data):
    centred = row_data - jnp.mean(row_data, axis=1, keepdims=True)
    inv_std = lax.rsqrt(jnp.mean(centred * centred, axis=1, keepdims=True) + epsilon)
    return (centred * inv_std, inv_std)


def norm_back(grad_in, normed, inv_std):
    return (
        grad_in
        - jnp.mean(grad_in, axis=1, keepdims=True)
        - normed * jnp.mean(grad_in * normed, axis=1, keepdims=True)
    ) * inv_std


def silu_slope(values):
    sigmoid_v = jax.nn.sigmoid(values)
    return sigmoid_v * (1.0 + values * (1.0 - sigmoid_v))


def history_starts(lengths, first_row, row_count):
    starts = jnp.cumsum(lengths) - lengths
    positions = first_row + jnp.arange(row_count, dtype=jnp.int32)
    owner_start = jnp.max(
        jnp.where(starts[None, :] <= positions[:, None], starts[None, :], 0), axis=1
    )
    return (owner_start, positions)


def visible(owner_start, positions, key_rows):
    allowed = (key_rows[None, :] >= owner_start[:, None]) & (
        key_rows[None, :] <= positions[:, None]
    )
    return allowed.astype(jnp.float32)


def shards(events, input_weight, output_weight, positives, negatives, log_probs, lengths):
    row_count, feature_width = events.shape
    head_size = feature_width // HEADS
    key_scale = 1.0 / math.sqrt(head_size)
    reach_count = REACH
    earlier_count = reach_count * row_count
    key_count = earlier_count + row_count
    first_row = lax.axis_index(("dp", "seq", "pool")) * row_count
    owner_start, positions = history_starts(lengths, first_row, row_count)
    key_rows = first_row - earlier_count + jnp.arange(key_count, dtype=jnp.int32)
    allowed = visible(owner_start, positions, key_rows)
    event_rows = events.astype(jnp.float32)
    normed_x, inv_x = normalize(event_rows)
    pre_act = jnp.dot(
        normed_x.astype(jnp.bfloat16), input_weight, preferred_element_type=jnp.float32
    )
    activated = jax.nn.silu(pre_act).astype(jnp.bfloat16)
    update_rows = activated[:, :feature_width]
    queries = activated[:, feature_width : 2 * feature_width]
    key_values = activated[:, 2 * feature_width :]
    earlier_blocks = []
    travelling = key_values
    for hop_index in range(reach_count):
        travelling = shifted(travelling, ("dp", "seq", "pool"), 1)
        earlier_blocks.append(travelling)
    kv_all = jnp.concatenate(earlier_blocks[::-1] + [key_values], axis=0)
    keys_all = kv_all[:, :feature_width]
    values_all = kv_all[:, feature_width:]
    query_heads = queries.reshape(row_count, HEADS, head_size)
    key_heads = keys_all.reshape(key_count, HEADS, head_size)
    value_heads = values_all.reshape(key_count, HEADS, head_size)
    scores = (
        jnp.einsum("ihd,jhd->hij", query_heads, key_heads, preferred_element_type=jnp.float32)
        * key_scale
    )
    weights = (jax.nn.silu(scores) * allowed[None] / EV_DEV).astype(jnp.bfloat16)
    mixed_out = jnp.einsum(
        "hij,jhd->ihd", weights, value_heads, preferred_element_type=jnp.float32
    ).reshape(row_count, feature_width)
    normed_o, inv_o = normalize(mixed_out)
    update32 = update_rows.astype(jnp.float32)
    gated_rows = (normed_o * update32).astype(jnp.bfloat16)
    layer_out = jnp.dot(gated_rows, output_weight, preferred_element_type=jnp.float32) + event_rows
    inv_norm = lax.rsqrt(jnp.sum(layer_out * layer_out, axis=1, keepdims=True))
    normalized_result_vector = layer_out * inv_norm
    unit_low = normalized_result_vector.astype(jnp.bfloat16)
    positive_rows = positives.astype(jnp.float32)
    target_normalized_vectors = positive_rows * lax.rsqrt(
        jnp.sum(positive_rows * positive_rows, axis=1, keepdims=True)
    )
    target_similarity = (
        jnp.sum(normalized_result_vector * target_normalized_vectors, axis=1) / sharpness_divisor
    )
    negative_rows = negatives.astype(jnp.float32)
    sampled_decoy_vectors = (
        negative_rows * lax.rsqrt(jnp.sum(negative_rows * negative_rows, axis=1, keepdims=True))
    ).astype(jnp.bfloat16)
    neg_piece = lax.all_gather(sampled_decoy_vectors, "pool", axis=0, tiled=True)
    offset_piece = lax.all_gather(log_probs, "pool", axis=0, tiled=True)
    similarity_values_matrix = (
        jnp.einsum("rd,nd->rn", unit_low, neg_piece, preferred_element_type=jnp.float32)
        / sharpness_divisor
        - offset_piece.astype(jnp.float32)[None, :]
    )
    exp_terms = jnp.exp(similarity_values_matrix)
    exp_total = jnp.sum(exp_terms, axis=1)
    probability_mixed_vectors = jnp.dot(
        exp_terms.astype(jnp.bfloat16), neg_piece, preferred_element_type=jnp.float32
    )
    target_exp_term = jnp.exp(target_similarity)
    partition_denominator = target_exp_term + exp_total
    derivative_normalized_matrix = (
        loss_multiplier
        / sharpness_divisor
        * (
            probability_mixed_vectors / partition_denominator[:, None]
            + (target_exp_term / partition_denominator - 1.0)[:, None] * target_normalized_vectors
        )
    )
    grad_out = (
        derivative_normalized_matrix
        - normalized_result_vector
        * jnp.sum(normalized_result_vector * derivative_normalized_matrix, axis=1, keepdims=True)
    ) * inv_norm
    grad_low = grad_out.astype(jnp.bfloat16)
    grad_gated = jnp.einsum(
        "re,de->rd", grad_low, output_weight, preferred_element_type=jnp.float32
    )
    grad_update = grad_gated * normed_o
    grad_normed = grad_gated * update32
    grad_mixed = norm_back(grad_normed, normed_o, inv_o).astype(jnp.bfloat16)
    grad_heads = grad_mixed.reshape(row_count, HEADS, head_size)
    grad_values = jnp.einsum(
        "hij,ihd->jhd", weights, grad_heads, preferred_element_type=jnp.float32
    ).reshape(key_count, feature_width)
    grad_weights = jnp.einsum(
        "ihd,jhd->hij", grad_heads, value_heads, preferred_element_type=jnp.float32
    )
    grad_scores = (grad_weights * allowed[None] / EV_DEV * silu_slope(scores)).astype(jnp.bfloat16)
    grad_query = (
        jnp.einsum(
            "hij,jhd->ihd", grad_scores, key_heads, preferred_element_type=jnp.float32
        ).reshape(row_count, feature_width)
        * key_scale
    )
    grad_keys = (
        jnp.einsum(
            "hij,ihd->jhd", grad_scores, query_heads, preferred_element_type=jnp.float32
        ).reshape(key_count, feature_width)
        * key_scale
    )
    grad_kv = jnp.concatenate([grad_keys, grad_values], axis=1)
    running = grad_kv[:row_count]
    for hop_index in range(reach_count):
        arrived = shifted(running, ("dp", "seq", "pool"), -1)
        running = arrived + grad_kv[(hop_index + 1) * row_count : (hop_index + 2) * row_count]
    grad_act = jnp.concatenate([grad_update, grad_query, running], axis=1)
    grad_pre = (grad_act * silu_slope(pre_act)).astype(jnp.bfloat16)
    grad_x = jnp.einsum("rf,df->rd", grad_pre, input_weight, preferred_element_type=jnp.float32)
    d_events = norm_back(grad_x, normed_x, inv_x) + grad_out
    partial_rows = lax.psum_scatter(
        jnp.einsum("rd,re->de", gated_rows, grad_low, preferred_element_type=jnp.float32),
        ("dp", "seq"),
        scatter_dimension=0,
        tiled=True,
    )
    d_output_weight = lax.psum(partial_rows, "pool")
    return (d_events, d_output_weight)


def solution(mesh):
    placed = (
        P(("dp", "seq", "pool"), None),
        P(),
        P(),
        P(("dp", "seq", "pool"), None),
        P("pool", None),
        P("pool"),
        P(),
    )
    return jax.shard_map(
        shards,
        mesh=mesh,
        in_specs=placed,
        out_specs=(P(("dp", "seq", "pool"), None), P(("dp", "seq"), None)),
        check_vma=False,
    )
```

profile of v0, /device:TPU:6, one launch (start us, length us, event | category | flops | bytes accessed | tf_op | source)
XLA Modules:
  0.0 386.2 jit_solution(16091044714947541631)
XLA Ops:
  7.2 1.2 fusion.31
  8.5 1.8 fusion.32
  10.3 1.1 convert_reduce_fusion
  11.4 1.2 fusion.28
  12.6 6.3 %multiply_convert_fusion = (bf16[128,4096]{1,0:T(8,128)(2,1)S(1)}, f32[128,4096]{1,0:T(8,128)}) fusion(bf16[1024,4096]{1,0:T(8,128)(2,1)} %param.8, bf16[128,1024]{1,0:T(8,128)(2,1)} %param.7, f32[128]{0:T(128)S(1)} %add_rsqrt_fusion.1, f32[128]{0:T(128)S(1)} %broadcast_multiply_fusion.5), kind=kOutput, calls=%fused_computation.9 | convolution fusion | flops 1076887552 | bytes 11797504 | tf_op jit(solution)/shard_map/dot_general | solution.py:72
  18.8 0.9 slice.41
  19.7 4.3 %collective-permute-start = (bf16[128,2048]{1,0:T(8,128)(2,1)}, bf16[128,2048]{1,0:T(8,128)(2,1)}, u32[]{:S(2)}, u32[]{:S(2)}) collective-permute-start(bf16[128,2048]{1,0:T(8,128)(2,1)} %slice.41), channel_id=1, source_target_pairs={{0,1},{1,2},{2,3},{3,4},{4,5},{5,6},{6,7},{7,8},{8,9},{9,10},{10,1... | collective-permute-start | bytes 1572872 | tf_op jit(solution)/shard_map/ppermute | solution.py:21
  24.0 0.7 slice.43
  25.3 1.1 copy.61
  26.4 45.0 %all-gather = bf16[12,1,128]{2,1,0:T(2,128)(2,1)S(1)} all-gather(bf16[1,1,128]{2,1,0:T(2,128)(2,1)S(1)} %bitcast.65), channel_id=1, replica_groups=mesh['dp'=16,'seq'=4,'pool'=12] {'pool'}, dimensions={0}, use_global_device_ids=true | all-gather | bytes 3328 | tf_op jit(solution)/shard_map/all_gather | solution.py:117
  71.5 1.9 collective-permute-start.1
  73.7 0.8 and_convert_fusion
  74.5 17.2 %collective-permute-done.1 = bf16[128,2048]{1,0:T(8,128)(2,1)S(1)} collective-permute-done((bf16[128,2048]{1,0:T(8,128)(2,1)}, bf16[128,2048]{1,0:T(8,128)(2,1)S(1)}, u32[]{:S(2)}, u32[]{:S(2)}) %collective-permute-start.1) | collective-permute-done | bytes 524320 | tf_op jit(solution)/shard_map/ppermute | solution.py:21
  91.8 1.3 pad_maximum_fusion
  93.1 1.4 slice_bitcast_fusion
  94.4 1.5 copy.62
  96.0 3.1 multiply_convert_fusion.2
  99.1 0.5 fusion.52
  100.4 1.2 fusion.30
  101.5 0.7 copy-done.13
  102.3 0.5 multiply_reduce_fusion.2
  103.1 3.3 fusion.53
  106.5 0.8 multiply_reduce_fusion.1
  107.3 1.2 subtract_multiply_fusion
  108.5 2.7 fusion.44
  111.3 1.9 fusion.43
  113.2 2.1 fusion.37
  115.2 1.1 copy.63
  116.4 2.5 multiply_convert_fusion.1
  118.9 0.9 copy-done.10
  119.8 1.6 convolution_multiply_fusion.1
  121.4 3.0 copy.59
  124.4 2.7 fusion.54
  127.1 3.1 copy.60
  130.3 1.4 fusion.9
  131.7 2.3 collective-permute-start.2
  134.0 21.6 %collective-permute-done.2 = f32[128,2048]{1,0:T(8,128)S(1)} collective-permute-done((f32[128,2048]{1,0:T(8,128)S(1)}, f32[128,2048]{1,0:T(8,128)S(1)}, u32[]{:S(2)}, u32[]{:S(2)}) %collective-permute-start.2) | collective-permute-done | bytes 1048608 | tf_op jit(solution)/shard_map/ppermute | solution.py:21
  155.6 1.1 fusion.8
  156.8 4.5 %collective-permute-start.3 = (f32[128,2048]{1,0:T(8,128)}, f32[128,2048]{1,0:T(8,128)}, u32[]{:S(2)}, u32[]{:S(2)}) collective-permute-start(f32[128,2048]{1,0:T(8,128)} %fusion.8), channel_id=1, source_target_pairs={{1,0},{2,1},{3,2},{4,3},{5,4},{6,5},{7,6},{8,7},{9,8},{10,9},{11,1... | collective-permute-start | bytes 3145736 | tf_op jit(solution)/shard_map/ppermute | solution.py:21
  161.3 0.5 convolution_multiply_fusion.3
  161.7 1.0 copy.58
  162.7 17.2 %collective-permute-done.3 = f32[128,2048]{1,0:T(8,128)} collective-permute-done((f32[128,2048]{1,0:T(8,128)}, f32[128,2048]{1,0:T(8,128)}, u32[]{:S(2)}, u32[]{:S(2)}) %collective-permute-start.3) | collective-permute-done | bytes 1048608 | tf_op jit(solution)/shard_map/ppermute | solution.py:21
  179.9 1.6 fusion.10
  181.6 7.1 %fusion.51 = (f32[128]{0:T(128)S(1)}, f32[128]{0:T(128)S(1)}, f32[128,1024]{1,0:T(8,128)}) fusion(f32[128]{0:T(128)S(1)} %add_rsqrt_fusion.1, f32[128]{0:T(128)S(1)} %broadcast_multiply_fusion.5, bf16[128,1024]{1,0:T(8,128)(2,1)S(1)} %copy-done.4, bf16[1024,4096]{1,0:T(8,128)(2,1)} %param.8, f32[128,2048]{1,0:T(8,128)S(1)} %fusion.10, ...), kind=kOutput, calls=%fused_computation.101 | convolution fusion | flops 1080295168 | bytes 13371392 | tf_op jit(solution)/shard_map/rf,df->rd/dot_general | solution.py:177
  188.7 77.3 %reduce-scatter.2.cloned.1.call-done = f32[16,1024]{1,0:T(8,128)} async-done(((f32[1024,1024]{1,0:T(8,128)}), f32[16,1024]{1,0:T(8,128)}) %reduce-scatter.2.cloned.1.call-update) | async-done | bytes 65552 | tf_op jit(solution)/shard_map/reduce_scatter | solution.py:179
  266.0 2.1 fusion.27
  268.1 110.1 %all-reduce.2.cloned.1.call-done = f32[16,1024]{1,0:T(8,128)} async-done(((f32[16,1024]{1,0:T(8,128)}), f32[16,1024]{1,0:T(8,128)}) %all-reduce.2.cloned.1.call-update) | async-done | bytes 65552 | tf_op jit(solution)/shard_map/psum | solution.py:185
  378.2 1.5 copy.76
  (80 shorter events, 2.3 us)
Async XLA Ops:
  7.2 95.1 %copy-start = (bf16[1024,1024]{1,0:T(8,128)(2,1)S(1)}, bf16[1024,1024]{1,0:T(8,128)(2,1)}, u32[]{:S(2)}) copy-start(bf16[1024,1024]{1,0:T(8,128)(2,1)} %param.9) | copy-start | bytes 6291460
  7.2 95.9 %all-gather.3.cloned.1.call-start = ((), (), s32[]{:S(2)}) async-start(), calls=%async_computation.1 | async-start | bytes 3407872 | tf_op jit(solution)/shard_map/all_gather | solution.py:116
  10.3 255.7 %reduce-scatter.2.cloned.1.call-start = ((), (), s32[]{:S(2)}) async-start(), calls=%async_computation.2 | async-start | bytes 4259840 | tf_op jit(solution)/shard_map/reduce_scatter | solution.py:179
  12.6 12.2 %copy-start.17 = (bf16[128,1024]{1,0:T(8,128)(2,1)S(1)}, bf16[128,1024]{1,0:T(8,128)(2,1)}, u32[]{:S(2)}) copy-start(bf16[128,1024]{1,0:T(8,128)(2,1)} %param.10) | copy-start | bytes 786436
  12.6 12.3 %copy-start.22 = (s32[768]{0:T(1024)S(1)}, s32[768]{0:T(1024)}, u32[]{:S(2)}) copy-start(s32[768]{0:T(1024)} %param.13) | copy-start | bytes 9220
  18.8 74.2 %copy-start.12 = (bf16[128,4096]{1,0:T(8,128)(2,1)}, bf16[128,4096]{1,0:T(8,128)(2,1)S(1)}, u32[]{:S(2)}) copy-start(bf16[128,4096]{1,0:T(8,128)(2,1)S(1)} %get-tuple-element.12) | copy-start | bytes 3145732
  18.8 7.6 %copy-start.23 = (bf16[128]{0:T(256)(128)(2,1)S(1)}, bf16[128]{0:T(256)(128)(2,1)}, u32[]{:S(2)}) copy-start(bf16[128]{0:T(256)(128)(2,1)} %param.12) | copy-start | bytes 772
  19.7 51.8 %collective-permute-start = (bf16[128,2048]{1,0:T(8,128)(2,1)}, bf16[128,2048]{1,0:T(8,128)(2,1)}, u32[]{:S(2)}, u32[]{:S(2)}) collective-permute-start(bf16[128,2048]{1,0:T(8,128)(2,1)} %slice.41), channel_id=1, source_target_pairs={{0,1},{1,2},{2,3},{3,4},{4,5},{5,6},{6,7},{7,8},{8,9},{9,10},{10,1... | collective-permute-start | bytes 1572872 | tf_op jit(solution)/shard_map/ppermute | solution.py:21
  26.4 69.6 %copy-start.15 = (bf16[128,1024]{0,1:T(8,128)(2,1)}, bf16[128,1024]{0,1:T(8,128)(2,1)S(1)}, u32[]{:S(2)}) copy-start(bf16[128,1024]{0,1:T(8,128)(2,1)S(1)} %copy.61) | copy-start | bytes 786436
  71.5 20.2 %collective-permute-start.1 = (bf16[128,2048]{1,0:T(8,128)(2,1)}, bf16[128,2048]{1,0:T(8,128)(2,1)S(1)}, u32[]{:S(2)}, u32[]{:S(2)}) collective-permute-start(bf16[128,2048]{1,0:T(8,128)(2,1)} %collective-permute-done), channel_id=1, source_target_pairs={{0,1},{1,2},{2,3},{3,4},{4,5},{5,6},{6,7},{7,8},{8,9},{9,10},{10,1... | collective-permute-start | bytes 1572872 | tf_op jit(solution)/shard_map/ppermute | solution.py:21
  95.9 3.2 copy-start.6
  95.9 3.2 copy-start.9
  99.1 0.9 copy-start.8
  99.1 3.2 copy-start.4
  100.4 2.4 copy-start.18
  101.5 0.7 copy-start.13
  102.8 3.7 copy-start.3
  103.1 3.4 copy-start.5
  103.1 3.4 copy-start.19
  106.5 2.0 copy-start.14
  111.2 267.0 %all-reduce.2.cloned.1.call-start = ((), (), s32[]{:S(2)}) async-start(), calls=%async_computation.3 | async-start | bytes 131072 | tf_op jit(solution)/shard_map/psum | solution.py:185
  116.4 3.5 copy-start.16
  118.9 0.9 copy-start.10
  130.3 25.4 %copy-start.1 = (f32[384,1024]{1,0:T(8,128)S(1)}, f32[384,1024]{1,0:T(8,128)}, u32[]{:S(2)}) copy-start(f32[384,1024]{1,0:T(8,128)} %copy.59) | copy-start | bytes 4718596
  130.3 25.4 %copy-start.2 = (f32[384,1024]{1,0:T(8,128)S(1)}, f32[384,1024]{1,0:T(8,128)}, u32[]{:S(2)}) copy-start(f32[384,1024]{1,0:T(8,128)} %copy.60) | copy-start | bytes 4718596
  131.7 29.5 %copy-start.7 = (bf16[384,1024]{0,1:T(8,128)(2,1)S(1)}, bf16[384,1024]{0,1:T(8,128)(2,1)}, u32[]{:S(2)}) copy-start(bf16[384,1024]{0,1:T(8,128)(2,1)} %copy-done.6) | copy-start | bytes 2359300
  131.7 29.5 %copy-start.11 = (bf16[8,128,384]{2,1,0:T(8,128)(2,1)S(1)}, bf16[8,128,384]{2,1,0:T(8,128)(2,1)}, u32[]{:S(2)}) copy-start(bf16[8,128,384]{2,1,0:T(8,128)(2,1)} %copy-done.10) | copy-start | bytes 2359300
  131.7 23.9 %collective-permute-start.2 = (f32[128,2048]{1,0:T(8,128)S(1)}, f32[128,2048]{1,0:T(8,128)S(1)}, u32[]{:S(2)}, u32[]{:S(2)}) collective-permute-start(f32[128,2048]{1,0:T(8,128)S(1)} %fusion.9), channel_id=1, source_target_pairs={{1,0},{2,1},{3,2},{4,3},{5,4},{6,5},{7,6},{8,7},{9,8},{10,9},{11,1... | collective-permute-start | bytes 3145736 | tf_op jit(solution)/shard_map/ppermute | solution.py:21
  156.8 23.2 %collective-permute-start.3 = (f32[128,2048]{1,0:T(8,128)}, f32[128,2048]{1,0:T(8,128)}, u32[]{:S(2)}, u32[]{:S(2)}) collective-permute-start(f32[128,2048]{1,0:T(8,128)} %fusion.8), channel_id=1, source_target_pairs={{1,0},{2,1},{3,2},{4,3},{5,4},{6,5},{7,6},{8,7},{9,8},{10,9},{11,1... | collective-permute-start | bytes 3145736 | tf_op jit(solution)/shard_map/ppermute | solution.py:21
  162.7 18.8 %copy-start.20 = (f32[128,1024]{1,0:T(8,128)S(1)}, f32[128,1024]{1,0:T(8,128)}, u32[]{:S(2)}) copy-start(f32[128,1024]{1,0:T(8,128)} %get-tuple-element.8) | copy-start | bytes 1572868
  162.7 18.8 %copy-start.21 = (f32[128,1024]{1,0:T(8,128)S(1)}, f32[128,1024]{1,0:T(8,128)}, u32[]{:S(2)}) copy-start(f32[128,1024]{1,0:T(8,128)} %copy.58) | copy-start | bytes 1572868
  162.7 18.9 %copy-start.24 = (f32[128,4096]{1,0:T(8,128)S(1)}, f32[128,4096]{1,0:T(8,128)}, u32[]{:S(2)}) copy-start(f32[128,4096]{1,0:T(8,128)} %get-tuple-element.13) | copy-start | bytes 6291460
Sparse Core Ops, SparseCore 0:
  10.4 80.4 all-gather.2
  111.3 154.6 reduce-scatter.1
  268.5 109.6 all-reduce.1
where the time goes:
time: 387 us; the launch traced here: 386 us
  waiting for transfers between devices  243 us (63%)
  blocking collectives  45 us (12%)
  matrix products  33.5 us (9%)
  other arithmetic  19.2 us (5%)
  local copies, waits for them, and re-layouts  17.8 us (5%)
  between operations  14.2 us (4%)
  starting transfers between devices  13.1 us (3%)
    psum x1, waiting for transfers between devices, shards(): d_output_weight = lax.psum(partial_rows, 'pool')  110 us
    reduce_scatter x1, waiting for transfers between devices, shards(): lax.psum_scatter(jnp.einsum('rd,re->de', gated_rows, grad_low, preferred_...  77.3 us
    ppermute x4, waiting for transfers between devices, shifted(): return lax.ppermute(x, axis, pairs)  56 us
    all_gather x1, blocking collectives, shards(): offset_piece = lax.all_gather(log_probs, 'pool', axis=0, tiled=True)  45 us
    ppermute x4, starting transfers between devices, shifted(): return lax.ppermute(x, axis, pairs)  12.9 us
  transfers between devices with their start and end apart: 7, of which 5 were waited for; matrix products, arithmetic and copies ran while one was open for 14% of the time, Pallas kernels for 0%

commit v1 on v0

v1 whole, which is shorter than its diff:
```python
import functools
import math

import jax
import jax.numpy as jnp
from jax import lax
from jax.experimental import pallas as pl
from jax.experimental.pallas import tpu as pltpu
from jax.sharding import PartitionSpec as P

HEADS = 8
EV_DEV = 128

epsilon = 1e-05
sharpness_divisor = 0.05
loss_multiplier = 8.0

MESH = pl.DeviceIdType.MESH
AXES = ("dp", "seq", "pool")
NT = (((1,), (1,)), ((), ()))
NN = (((1,), (0,)), ((), ()))
HALVES = 2
F32 = jnp.float32
BF16 = jnp.bfloat16


def dot(a, b, dims=NN):
    return lax.dot_general(a, b, dims, preferred_element_type=F32)


def slope(v):
    sg = jax.nn.sigmoid(v)
    return sg * (1.0 + v * (1.0 - sg))


def mean_last(v):
    return jnp.mean(v, axis=1, keepdims=True)


def normalize(row_data):
    centred = row_data - mean_last(row_data)
    inv_std = lax.rsqrt(mean_last(centred * centred) + epsilon)
    return centred * inv_std, inv_std


def norm_back(grad_in, normed, inv_std):
    return (grad_in - mean_last(grad_in) - normed * mean_last(grad_in * normed)) * inv_std


def kernel(
    sizes,
    lens_ref,
    lp_ref,
    ev_hbm,
    win_hbm,
    wout_hbm,
    pos_hbm,
    neg_hbm,
    dev_hbm,
    dw_ref,
    ev,
    win,
    wout,
    pos,
    negs_raw,
    xn,
    normed_x,
    slopes,
    upd,
    qb,
    kb,
    vb,
    mask_f,
    mask_t,
    sc_slope,
    mixed,
    neg,
    lpb,
    ebuf,
    unit,
    gout,
    gl2,
    gt,
    gt_sib,
    gm,
    gact,
    gpre,
    dout,
    send_a,
    recv_x,
    own_b,
    send_b,
    recv_y,
    own_c,
    send_c,
    recv_z,
    fin,
    load_sem,
    halo_s,
    halo_r,
    gm_s,
    gm_r,
    ring_s,
    ring_r,
    xs_s,
    xs_r,
    sib_s,
    sib_r,
    lp_s,
    lp_r,
    pair_s,
    pair_r,
    dwx_s,
    dwx_r,
    dwy_s,
    dwy_r,
    dwz_s,
    dwz_r,
    fin_s,
    fin_r,
):
    ny, nx, nz, width, heads, events_all = sizes
    hw = width // heads
    rows = EV_DEV
    cb = 256
    ups, dns = nz // 2, nz - 1 - nz // 2
    reds = fin.shape[0]
    tw = fin.shape[2]
    out_rows = fin.shape[1]
    scale = 1.0 / math.sqrt(hw)

    dp = lax.axis_index("dp")
    sx = lax.axis_index("seq")
    pz = lax.axis_index("pool")
    core = lax.rem(dp, 2)
    yy = lax.div(dp, 2)
    other = dp + 1 - 2 * core
    total = 2 * ny * nx * nz
    me = (dp * nx + sx) * nz + pz

    def place(i):
        return (lax.div(i, nx * nz), lax.rem(lax.div(i, nz), nx), lax.rem(i, nz))

    nxt = place(lax.rem(me + 1, total))
    prv = place(lax.rem(me + total - 1, total))
    sib = (other, sx, pz)

    def at_x(d):
        return (dp, lax.rem(sx + d, nx), pz)

    def at_y(d):
        return (lax.rem(yy + d, ny) * 2 + core, sx, pz)

    def at_z(d):
        return (dp, sx, lax.rem(pz + d, nz))

    def load(i, src, dst):
        return pltpu.make_async_copy(src, dst, load_sem.at[i])

    def remote(src, dst, s, r, dev):
        return pltpu.make_async_remote_copy(
            src_ref=src, dst_ref=dst, send_sem=s, recv_sem=r, device_id=dev, device_id_type=MESH
        )

    loads = [
        load(0, neg_hbm, negs_raw),
        load(1, ev_hbm, ev),
        load(2, win_hbm.at[:, pl.ds(2 * width, width)], win.at[2]),
        load(3, win_hbm.at[:, pl.ds(3 * width, width)], win.at[3]),
        load(4, win_hbm.at[:, pl.ds(width, width)], win.at[1]),
        load(5, win_hbm.at[:, pl.ds(0, width)], win.at[0]),
        load(6, wout_hbm, wout),
        load(7, pos_hbm, pos),
    ]
    for item in loads:
        item.start()

    barrier = pltpu.get_barrier_semaphore()
    partners = [nxt, prv, sib]
    partners += [at_x(d) for d in range(1, nx)]
    partners += [at_y(d) for d in range(1, ny)]
    partners += [at_z(d) for d in range(1, nz)]
    for partner in partners:
        pl.semaphore_signal(barrier, inc=1, device_id=partner, device_id_type=MESH)

    half = rows // HALVES

    def halo(kind, p):
        a, b, dev = ((2, 1, nxt), (2, 3, prv), (1, 0, nxt), (3, 4, prv))[kind]
        part = pl.ds(p * half, half)
        return remote(
            xn.at[a, part], xn.at[b, part], halo_s.at[kind, p], halo_r.at[kind, p], dev
        )

    def gm_hop(kind, p):
        part = pl.ds(p * half, half)
        return remote(
            gm.at[kind, part], gm.at[kind + 1, part], gm_s.at[kind, p], gm_r.at[kind, p], prv
        )

    piece = core * nx + sx

    def shard_at(way, s):
        return lax.rem(pz - s + nz, nz) if way == 0 else lax.rem(pz + s, nz)

    def ring(way, s):
        ref = neg.at[shard_at(way, s), piece]
        return remote(
            ref, ref, ring_s.at[way, s], ring_r.at[way, s], at_z(1) if way == 0 else at_z(nz - 1)
        )

    def ring_arrived(way, s):
        ref = neg.at[shard_at(way, s + 1), piece]
        dev = at_z(1) if way == 0 else at_z(nz - 1)
        return remote(ref, ref, ring_s.at[way, s], ring_r.at[way, s], dev)

    def cross(way, s, d):
        ref = neg.at[shard_at(way, s + 1), piece]
        return remote(ref, ref, xs_s.at[way, s, d - 1], xs_r.at[way, s, d - 1], at_x(d))

    def cross_arrived(way, s, d):
        from_x = core * nx + lax.rem(sx - d + nx, nx)
        ref = neg.at[shard_at(way, s + 1), from_x]
        return remote(ref, ref, xs_s.at[way, s, d - 1], xs_r.at[way, s, d - 1], at_x(d))

    def sib_copy(way, s):
        ref = neg.at[shard_at(way, s + 1), pl.ds(core * nx, nx)]
        return remote(ref, ref, sib_s.at[way, s], sib_r.at[way, s], sib)

    def sib_arrived(way, s):
        ref = neg.at[shard_at(way, s + 1), pl.ds((1 - core) * nx, nx)]
        return remote(ref, ref, sib_s.at[way, s], sib_r.at[way, s], sib)

    def lp_copy(d):
        return remote(lpb.at[pz], lpb.at[pz], lp_s.at[d - 1], lp_r.at[d - 1], at_z(d))

    def lp_arrived(d):
        ref = lpb.at[lax.rem(pz - d + nz, nz)]
        return remote(ref, ref, lp_s.at[d - 1], lp_r.at[d - 1], at_z(d))

    loads[0].wait()
    raw = negs_raw[...].astype(F32)
    unit_neg = raw * lax.rsqrt(jnp.sum(raw * raw, axis=1, keepdims=True))
    neg[pz] = unit_neg.astype(BF16).reshape(neg.shape[1:])
    lpb[pz] = lp_ref[...]
    loads[1].wait()
    own_x, inv_x = normalize(ev[...].astype(F32))
    normed_x[...] = own_x
    xn[2] = own_x.astype(BF16)

    pl.semaphore_wait(barrier, len(partners))

    for p in range(HALVES):
        halo(0, p).start()
        halo(1, p).start()
    ring(0, 0).start()
    if dns:
        ring(1, 0).start()
    for d in range(1, nz):
        lp_copy(d).start()

    def serve(way, s):
        ring_arrived(way, s).wait_recv()
        if s + 1 < (ups, dns)[way]:
            ring(way, s + 1).start()
        for d in range(1, nx):
            cross(way, s, d).start()

    served = [0]

    def serve_next(count=1):
        for _ in range(count):
            s = served[0]
            for way in (0, 1):
                if s < (ups, dns)[way]:
                    serve(way, s)
            served[0] = s + 1

    def project_own(chunk, dst):
        def body(j, carry):
            cols = pl.ds(pl.multiple_of(j * cb, cb), cb)
            pre = dot(xn[2], win[chunk, :, cols])
            sg = jax.nn.sigmoid(pre)
            slopes[chunk, :, cols] = sg * (1.0 + pre * (1.0 - sg))
            dst[:, cols] = (pre * sg).astype(BF16)
            return carry

        lax.fori_loop(0, width // cb, body, 0)

    def project(slot, chunk, dst):
        def body(j, carry):
            cols = pl.ds(pl.multiple_of(j * cb, cb), cb)
            pre = dot(xn[slot], win[chunk, :, cols])
            dst[:, cols] = (pre * jax.nn.sigmoid(pre)).astype(BF16)
            return carry

        lax.fori_loop(0, width // cb, body, 0)

    loads[2].wait()
    project_own(2, kb.at[2])
    loads[3].wait()
    project_own(3, vb.at[2])

    for p in range(HALVES):
        halo(0, p).wait_recv()
        halo(2, p).start()
        halo(1, p).wait_recv()
        halo(3, p).start()
    serve_next()

    loads[4].wait()
    project_own(1, qb.at[0])
    loads[5].wait()
    project_own(0, upd)
    serve_next()

    users = lens_ref.shape[1]
    lens8 = lens_ref[...].astype(BF16)
    ri = lax.broadcasted_iota(jnp.int32, (users, users), 0)
    ci = lax.broadcasted_iota(jnp.int32, (users, users), 1)
    before_cols = (ri < ci).astype(F32).astype(BF16)
    before_rows = (ci < ri).astype(F32).astype(BF16)
    starts_row = dot(lens8, before_cols)[0:1, :]
    starts_col = dot(before_rows, lens8, NT)[:, 0:1]
    first = (me * rows).astype(F32)
    own_pos = first + lax.broadcasted_iota(jnp.int32, (rows, 1), 0).astype(F32)
    own_first = jnp.max(jnp.where(starts_row <= own_pos, starts_row, 0.0), axis=1, keepdims=True)
    key_pos = first - 2.0 * rows + lax.broadcasted_iota(jnp.int32, (rows, 3 * rows), 1).astype(F32)
    mask_f[...] = jnp.where((key_pos >= own_first) & (key_pos <= own_pos), 1.0 / EV_DEV, 0.0)
    row_pos = first + lax.broadcasted_iota(jnp.int32, (1, 3 * rows), 1).astype(F32)
    row_first = jnp.max(jnp.where(starts_col <= row_pos, starts_col, 0.0), axis=0, keepdims=True)
    row_first = jnp.where(row_pos < events_all, row_first, float(2 * events_all))
    mask_t[...] = jnp.where((own_pos >= row_first) & (own_pos <= row_pos), 1.0 / EV_DEV, 0.0)
    serve_next()

    project(1, 2, kb.at[1])
    project(1, 3, vb.at[1])
    serve_next()
    project(3, 1, qb.at[1])
    serve_next()
    for p in range(HALVES):
        halo(2, p).wait_recv()
    project(0, 2, kb.at[0])
    project(0, 3, vb.at[0])
    serve_next(max(ups - 5, 0))

    def head_forward(h, carry):
        cols = pl.ds(pl.multiple_of(h * hw, hw), hw)
        keys = kb[:, :, cols].reshape(3 * rows, hw)
        values = vb[:, :, cols].reshape(3 * rows, hw)
        s = dot(qb[0, :, cols], keys, NT) * scale
        sg = jax.nn.sigmoid(s)
        seen = mask_f[...]
        sc_slope[h] = seen * (sg * (1.0 + s * (1.0 - sg)))
        w = (s * sg * seen).astype(BF16)
        mixed[:, cols] = dot(w, values)
        return carry

    lax.fori_loop(0, heads, head_forward, 0)

    for way in (0, 1):
        for s in range((ups, dns)[way]):
            for d in range(1, nx):
                cross_arrived(way, s, d).wait_recv()
            sib_copy(way, s).start()

    normed_o, inv_o = normalize(mixed[...])
    mixed[...] = normed_o
    gated = normed_o * upd[...].astype(F32)
    gated_low = gated.astype(BF16)
    x_rows = ev[...].astype(F32)
    loads[6].wait()
    layer_out = dot(gated_low, wout[...]) + x_rows
    inv_norm = lax.rsqrt(jnp.sum(layer_out * layer_out, axis=1, keepdims=True))
    unit_out = layer_out * inv_norm
    unit[...] = unit_out
    unit_low = unit_out.astype(BF16)

    per_y = width // ny
    for j in range(ny):
        turned = gated[:, j * per_y : (j + 1) * per_y].T.astype(BF16)
        for c in range(2):
            for k in range(nx):
                r0 = (c * nx + k) * out_rows
                gt[c, k, j] = turned[r0 : r0 + out_rows]
    to_sib_g = remote(gt.at[1 - core], gt_sib, pair_s.at[0], pair_r.at[0], sib)
    to_sib_g.start()

    loads[7].wait()
    pos_rows = pos[...].astype(F32)
    pos_unit = pos_rows * lax.rsqrt(jnp.sum(pos_rows * pos_rows, axis=1, keepdims=True))
    pos_exp = jnp.exp(jnp.sum(unit_out * pos_unit, axis=1, keepdims=True) / sharpness_divisor)

    for d in range(1, nz):
        lp_arrived(d).wait_recv()
    for way in (0, 1):
        for s in range((ups, dns)[way]):
            sib_arrived(way, s).wait_recv()

    def logits(z, exp_total):
        negs = neg[z].reshape(rows, width)
        lg = dot(unit_low, negs, NT) * (1.0 / sharpness_divisor) - lpb[z, 0:1, :]
        e = jnp.exp(lg)
        ebuf[:, pl.ds(pl.multiple_of(z * rows, rows), rows)] = e.astype(BF16)
        return exp_total + jnp.sum(e, axis=1, keepdims=True)

    exp_total = lax.fori_loop(0, nz, logits, jnp.zeros((rows, 1), F32))
    denominator = pos_exp + exp_total
    mixed_negs = dot(ebuf[...], neg[...].reshape(nz * rows, width))
    unit_out = unit[...]
    grad_unit = (
        loss_multiplier
        / sharpness_divisor
        * (mixed_negs / denominator + (pos_exp / denominator - 1.0) * pos_unit)
    )
    grad_out = (
        grad_unit - unit_out * jnp.sum(unit_out * grad_unit, axis=1, keepdims=True)
    ) * inv_norm
    gout[...] = grad_out
    gl2[0] = grad_out.astype(BF16)
    to_sib_l = remote(gl2.at[0], gl2.at[1], pair_s.at[1], pair_r.at[1], sib)
    to_sib_l.start()

    def gate_back(j, carry):
        cols = pl.ds(pl.multiple_of(j * cb, cb), cb)
        gact[:, cols] = dot(gl2[0], wout[cols, :], NT)
        return carry

    lax.fori_loop(0, width // cb, gate_back, 0)
    grad_gated = gact[...]
    normed_o = mixed[...]
    gpre[:, 0:width] = (grad_gated * normed_o * slopes[0]).astype(BF16)
    gm[0] = norm_back(grad_gated * upd[...].astype(F32), normed_o, inv_o).astype(BF16)
    for p in range(HALVES):
        gm_hop(0, p).start()

    to_sib_g.wait_recv()
    to_sib_l.wait_recv()

    def weight_part(k):
        mine = gt[core, k].reshape(ny * out_rows, rows)
        theirs = gt_sib[k].reshape(ny * out_rows, rows)
        left = jnp.concatenate([mine, theirs], axis=1)
        return dot(left, gl2[...].reshape(2 * rows, width))

    def dwx(d):
        return remote(
            send_a.at[d - 1], recv_x.at[d - 1], dwx_s.at[d - 1], dwx_r.at[d - 1], at_x(d)
        )

    for d in range(1, nx):
        send_a[d - 1] = weight_part(lax.rem(sx + d, nx)).astype(BF16).reshape(send_a.shape[1:])
        dwx(d).start()
    own_b[...] = weight_part(sx).reshape(own_b.shape)

    def head_query(h, carry):
        cols = pl.ds(pl.multiple_of(h * hw, hw), hw)
        values = vb[:, :, cols].reshape(3 * rows, hw)
        keys = kb[:, :, cols].reshape(3 * rows, hw)
        gs = (dot(gm[0, :, cols], values, NT) * sc_slope[h]).astype(BF16)
        gq = dot(gs, keys) * scale
        at = pl.ds(pl.multiple_of(width + h * hw, hw), hw)
        gpre[:, at] = (gq * slopes[1, :, cols]).astype(BF16)
        return carry

    lax.fori_loop(0, heads, head_query, 0)

    for p in range(HALVES):
        gm_hop(0, p).wait_recv()
        gm_hop(1, p).start()

    for p in range(HALVES):
        halo(3, p).wait_recv()
    project(4, 1, qb.at[2])

    def dwy(d):
        return remote(
            send_b.at[lax.rem(yy + d, ny)], recv_y.at[d - 1], dwy_s.at[d - 1], dwy_r.at[d - 1], at_y(d)
        )

    for d in range(1, nx):
        dwx(d).wait_recv()
    summed = own_b[...]
    for d in range(1, nx):
        summed = summed + recv_x[d - 1].astype(F32)
    own_b[...] = summed
    send_b[...] = summed.astype(BF16)
    for d in range(1, ny):
        dwy(d).start()

    for p in range(HALVES):
        gm_hop(1, p).wait_recv()

    def head_keys(h, carry):
        cols = pl.ds(pl.multiple_of(h * hw, hw), hw)
        queries = qb[:, :, cols].reshape(3 * rows, hw)
        grads = gm[:, :, cols].reshape(3 * rows, hw)
        s = dot(kb[2, :, cols], queries, NT) * scale
        sg = jax.nn.sigmoid(s)
        seen = mask_t[...]
        w = (s * sg * seen).astype(BF16)
        gv = dot(w, grads)
        gs = (dot(vb[2, :, cols], grads, NT) * seen * (sg * (1.0 + s * (1.0 - sg)))).astype(BF16)
        gk = dot(gs, queries) * scale
        at = pl.ds(pl.multiple_of(2 * width + h * hw, hw), hw)
        gpre[:, at] = (gk * slopes[2, :, cols]).astype(BF16)
        at = pl.ds(pl.multiple_of(3 * width + h * hw, hw), hw)
        gpre[:, at] = (gv * slopes[3, :, cols]).astype(BF16)
        return carry

    lax.fori_loop(0, heads, head_keys, 0)

    def dwz(d):
        return remote(
            send_c.at[lax.rem(pz + d, nz)], recv_z.at[d - 1], dwz_s.at[d - 1], dwz_r.at[d - 1], at_z(d)
        )

    def dwz_arrived(d):
        return remote(send_c.at[0], recv_z.at[d - 1], dwz_s.at[d - 1], dwz_r.at[d - 1], at_z(d))

    def fin_copy(d):
        return remote(fin.at[pz], fin.at[pz], fin_s.at[d - 1], fin_r.at[d - 1], at_z(d))

    def fin_arrived(d):
        ref = fin.at[lax.rem(pz - d + nz, nz)]
        return remote(ref, ref, fin_s.at[d - 1], fin_r.at[d - 1], at_z(d))

    for d in range(1, ny):
        dwy(d).wait_recv()
    summed = own_b[yy]
    for d in range(1, ny):
        summed = summed + recv_y[d - 1].astype(F32)
    for t in range(reds):
        own_c[t] = summed[:, t * tw : (t + 1) * tw]
        send_c[t] = summed[:, t * tw : (t + 1) * tw].astype(BF16)
    for d in range(1, nz):

        @pl.when(lax.rem(pz + d, nz) < reds)
        def _(d=d):
            dwz(d).start()

    def x_back(j, carry):
        cols = pl.ds(pl.multiple_of(j * cb, cb), cb)
        part = dot(gpre[:, 0:width], win[0, cols, :], NT)
        for c in range(1, 4):
            part = part + dot(gpre[:, c * width : (c + 1) * width], win[c, cols, :], NT)
        gact[:, cols] = part
        return carry

    lax.fori_loop(0, width // cb, x_back, 0)

    @pl.when(pz < reds)
    def _():
        for d in range(1, nz):
            dwz_arrived(d).wait_recv()
        done = own_c[pz]
        for d in range(1, nz):
            done = done + recv_z[d - 1].astype(F32)
        fin[pz] = done
        for d in range(1, nz):
            fin_copy(d).start()

    dout[...] = norm_back(gact[...], normed_x[...], inv_x) + gout[...]
    out_copy = pltpu.make_async_copy(dout, dev_hbm, load_sem.at[8])
    out_copy.start()

    for d in range(1, nz):

        @pl.when(lax.rem(pz - d + nz, nz) < reds)
        def _(d=d):
            fin_arrived(d).wait_recv()

    for t in range(reds):
        dw_ref[:, t * tw : (t + 1) * tw] = fin[t]
    out_copy.wait()

    for p in range(HALVES):
        for kind in range(4):
            halo(kind, p).wait_send()
        for kind in range(2):
            gm_hop(kind, p).wait_send()
    for way in (0, 1):
        for s in range((ups, dns)[way]):
            ring(way, s).wait_send()
            for d in range(1, nx):
                cross(way, s, d).wait_send()
            sib_copy(way, s).wait_send()
    for d in range(1, nz):
        lp_copy(d).wait_send()
    to_sib_g.wait_send()
    to_sib_l.wait_send()
    for d in range(1, nx):
        dwx(d).wait_send()
    for d in range(1, ny):
        dwy(d).wait_send()
    for d in range(1, nz):

        @pl.when(lax.rem(pz + d, nz) < reds)
        def _(d=d):
            dwz(d).wait_send()

    @pl.when(pz < reds)
    def _():
        for d in range(1, nz):
            fin_copy(d).wait_send()


def shards(mesh_sizes, events, input_weight, output_weight, positives, negatives, log_probs, lengths):
    ndp, nx, nz = mesh_sizes
    ny = ndp // 2
    rows, width = events.shape
    heads = HEADS
    users = lengths.shape[0]
    ups = nz // 2
    reds = 8 if nz >= 8 else 2
    tw = width // reds
    out_rows = width // (ndp * nx)
    piece_rows = rows // (2 * nx)
    events_all = rows * ndp * nx * nz
    lens8 = jnp.broadcast_to(lengths.astype(F32)[None, :], (8, users))
    lp8 = jnp.broadcast_to(log_probs.astype(F32)[None, :], (8, rows))
    v = pltpu.VMEM
    dma = pltpu.SemaphoreType.DMA
    scratch = [
        v((rows, width), BF16),
        v((4, width, width), BF16),
        v((width, width), BF16),
        v((rows, width), BF16),
        v((rows, width), BF16),
        v((5, rows, width), BF16),
        v((rows, width), F32),
        v((4, rows, width), F32),
        v((rows, width), BF16),
        v((3, rows, width), BF16),
        v((3, rows, width), BF16),
        v((3, rows, width), BF16),
        v((rows, 3 * rows), F32),
        v((rows, 3 * rows), F32),
        v((heads, rows, 3 * rows), F32),
        v((rows, width), F32),
        v((nz, 2 * nx, piece_rows, width), BF16),
        v((nz, 8, rows), F32),
        v((rows, nz * rows), BF16),
        v((rows, width), F32),
        v((rows, width), F32),
        v((2, rows, width), BF16),
        v((2, nx, ny, out_rows, rows), BF16),
        v((nx, ny, out_rows, rows), BF16),
        v((3, rows, width), BF16),
        v((rows, width), F32),
        v((rows, 4 * width), BF16),
        v((rows, width), F32),
        v((nx - 1, ny, out_rows, width), BF16),
        v((nx - 1, ny, out_rows, width), BF16),
        v((ny, out_rows, width), F32),
        v((ny, out_rows, width), BF16),
        v((ny - 1, out_rows, width), BF16),
        v((reds, out_rows, tw), F32),
        v((reds, out_rows, tw), BF16),
        v((nz - 1, out_rows, tw), BF16),
        v((reds, out_rows, tw), F32),
        dma((9,)),
        dma((4, HALVES)),
        dma((4, HALVES)),
        dma((2, HALVES)),
        dma((2, HALVES)),
        dma((2, ups)),
        dma((2, ups)),
        dma((2, ups, nx - 1)),
        dma((2, ups, nx - 1)),
        dma((2, ups)),
        dma((2, ups)),
        dma((nz - 1,)),
        dma((nz - 1,)),
        dma((2,)),
        dma((2,)),
        dma((nx - 1,)),
        dma((nx - 1,)),
        dma((ny - 1,)),
        dma((ny - 1,)),
        dma((nz - 1,)),
        dma((nz - 1,)),
        dma((nz - 1,)),
        dma((nz - 1,)),
    ]
    hbm = pl.BlockSpec(memory_space=pl.ANY)
    vmem = pl.BlockSpec(memory_space=pltpu.VMEM)
    return pl.pallas_call(
        functools.partial(kernel, (ny, nx, nz, width, heads, events_all)),
        out_shape=(
            jax.ShapeDtypeStruct((rows, width), F32),
            jax.ShapeDtypeStruct((out_rows, width), F32),
        ),
        in_specs=[vmem, vmem, hbm, hbm, hbm, hbm, hbm],
        out_specs=(hbm, vmem),
        scratch_shapes=scratch,
        compiler_params=pltpu.CompilerParams(
            collective_id=0, has_side_effects=True, vmem_limit_bytes=56 * 1024 * 1024
        ),
    )(lens8, lp8, events, input_weight, output_weight, positives, negatives)


def solution(mesh):
    sizes = tuple(mesh.shape[a] for a in AXES)
    placed = (
        P(AXES, None),
        P(),
        P(),
        P(AXES, None),
        P("pool", None),
        P("pool"),
        P(),
    )
    return jax.shard_map(
        functools.partial(shards, sizes),
        mesh=mesh,
        in_specs=placed,
        out_specs=(P(AXES, None), P(("dp", "seq"), None)),
        check_vma=False,
    )
```

time: 387 us -> 117 us (0.30)
  waiting for transfers between devices: 243 us -> 0 us
  Pallas kernels: 0 us -> 110 us
  blocking collectives: 45 us -> 0 us
  matrix products: 33.5 us -> 0 us
  other arithmetic: 19.2 us -> 0.69 us
  between operations: 14.2 us -> 0.64 us
  starting transfers between devices: 13.1 us -> 0 us
  local copies, waits for them, and re-layouts: 17.8 us -> 5.22 us
    psum x1 -> x0, waiting for transfers between devices: 110 us -> none  [shards(): d_output_weight = lax.psum(partial_rows, 'pool')]
    pallas_call x0 -> x1, Pallas kernels: none -> 110 us  [shards(): pl.pallas_call(functools.partial(kernel, (ny, nx, nz, width, heads, event...]
    reduce_scatter x1 -> x0, waiting for transfers between devices: 77.3 us -> none  [shards(): lax.psum_scatter(jnp.einsum('rd,re->de', gated_rows, grad_low, preferred_...]
    ppermute x4 -> x0, waiting for transfers between devices: 56 us -> none  [shifted(): return lax.ppermute(x, axis, pairs)]
    all_gather x1 -> x0, blocking collectives: 45 us -> none  [shards(): offset_piece = lax.all_gather(log_probs, 'pool', axis=0, tiled=True)]
    dot_general x13 -> x0, matrix products: 33.5 us -> none  [the longest x1 7.14 us: shards(): jnp.einsum('rf,df->rd', grad_pre, input_weight, preferred_element_type=jn...]
    ppermute x4 -> x0, starting transfers between devices: 12.9 us -> none  [shifted(): return lax.ppermute(x, axis, pairs)]
    reshape x5 -> x0, local copies, waits for them, and re-layouts: 7.04 us -> none  [the longest x1 3.13 us: shards(): grad_values = jnp.einsum('hij,ihd->jhd', weights, grad_heads, preferred_e...]
  transfers between devices with their start and end apart: 7 -> 0, of which waited for: 5 -> 0; matrix products, arithmetic and copies ran while one was open for 14% -> 0% of each run, Pallas kernels for 0% -> 0%
where the time goes in v1:
time: 117 us; the launch traced here: 116 us
  Pallas kernels  110 us (94%)
  local copies, waits for them, and re-layouts  5.22 us (4%)
    pallas_call x1, Pallas kernels, shards(): pl.pallas_call(functools.partial(kernel, (ny, nx, nz, width, heads, event...  110 us
    unnamed x2, local copies, waits for them, and re-layouts  3.36 us

profile of v1, /device:TPU:6, one launch (start us, length us, event | category | flops | bytes accessed | tf_op | source)
XLA Modules:
  0.0 116.2 jit_solution(4248587917938272740)
XLA Ops:
  0.6 1.2 %broadcast_in_dim.5.lp_ref = f32[8,128]{1,0:T(8,128)} broadcast(bf16[128]{0:T(256)(128)(2,1)} %param.12), dimensions={1} | broadcast | bytes 4352 | tf_op jit(solution)/shard_map/broadcast_in_dim | solution.py:621
  1.9 0.7 convert_element_type.6
  2.6 0.6 broadcast_in_dim.4.lens_ref
  3.2 109.7 %shard_map.86 = (f32[128,1024]{1,0:T(8,128)}, f32[16,1024]{1,0:T(8,128)}) custom-call(f32[8,768]{1,0:T(8,128)} %broadcast_in_dim.4.lens_ref, f32[8,128]{1,0:T(8,128)} %broadcast_in_dim.5.lp_ref, bf16[128,1024]{1,0:T(8,128)(2,1)} %ev_hbm.1, bf16[1024,4096]{1,0:T(8,128)(2,1)} %win_hbm.1, bf16[1024,1024]{1,0:T(8,128)(2,1)} %wout_hbm.1, ...), custom_call_target="tpu_custom_call" | custom-call | tf_op jit(solution)/shard_map/pallas_call | solution.py:688
  112.9 1.9 %copy.11 = f32[128,1024]{1,0:T(8,128)} copy(f32[128,1024]{1,0:T(8,128)} %get-tuple-element.4) | data formatting | bytes 1048576
  114.7 1.5 %copy.12 = f32[16,1024]{1,0:T(8,128)} copy(f32[16,1024]{1,0:T(8,128)} %get-tuple-element.5) | data formatting | bytes 131072

commit v2 on v1

--- a/solution.py
+++ b/solution.py
@@ -86,8 +86,13 @@
     gact,
     gpre,
     dout,
+    gkeys,
+    gvals,
     send_a,
     recv_x,
+    send_a2,
+    recv_x2,
+    part_x,
     own_b,
     send_b,
     recv_y,
@@ -145,8 +150,10 @@
     prv = place(lax.rem(me + total - 1, total))
     sib = (other, sx, pz)
 
-    def at_x(d):
-        return (dp, lax.rem(sx + d, nx), pz)
+    xa = sx + 1 - 2 * lax.rem(sx, 2)
+    xb = nx - 1 - sx
+    dev_a = (dp, xa, pz)
+    dev_b = (dp, xb, pz)
 
     def at_y(d):
         return (lax.rem(yy + d, ny) * 2 + core, sx, pz)
@@ -177,7 +184,7 @@
 
     barrier = pltpu.get_barrier_semaphore()
     partners = [nxt, prv, sib]
-    partners += [at_x(d) for d in range(1, nx)]
+    partners += [dev_a, dev_b]
     partners += [at_y(d) for d in range(1, ny)]
     partners += [at_z(d) for d in range(1, nz)]
     for partner in partners:
@@ -214,14 +221,25 @@
         dev = at_z(1) if way == 0 else at_z(nz - 1)
         return remote(ref, ref, ring_s.at[way, s], ring_r.at[way, s], dev)
 
-    def cross(way, s, d):
-        ref = neg.at[shard_at(way, s + 1), piece]
-        return remote(ref, ref, xs_s.at[way, s, d - 1], xs_r.at[way, s, d - 1], at_x(d))
-
-    def cross_arrived(way, s, d):
-        from_x = core * nx + lax.rem(sx - d + nx, nx)
-        ref = neg.at[shard_at(way, s + 1), from_x]
-        return remote(ref, ref, xs_s.at[way, s, d - 1], xs_r.at[way, s, d - 1], at_x(d))
+    def cross(way, s, k):
+        to_a = (way == 0) == (k == 0)
+        z = shard_at(way, s + 1)
+        if way == 0 and k == 1:
+            ref = neg.at[z, pl.ds(core * nx + 2 * lax.div(sx, 2), 2)]
+        else:
+            ref = neg.at[z, core * nx + (sx, sx, xb)[k]]
+        return remote(ref, ref, xs_s.at[way, s, k], xs_r.at[way, s, k], dev_a if to_a else dev_b)
+
+    def cross_arrived(way, s, k):
+        z = shard_at(way, s + 1)
+        if way == 0:
+            ref = neg.at[z, core * nx + xa] if k == 0 else neg.at[z, pl.ds(core * nx + 2 * lax.div(xb, 2), 2)]
+        else:
+            ref = neg.at[z, core * nx + (xb, xa, nx - 1 - xa)[k]]
+        to_a = (way == 0) == (k == 0)
+        return remote(ref, ref, xs_s.at[way, s, k], xs_r.at[way, s, k], dev_a if to_a else dev_b)
+
+    hops = ((1,), (1, 2))
 
     def sib_copy(way, s):
         ref = neg.at[shard_at(way, s + 1), pl.ds(core * nx, nx)]
@@ -242,7 +260,7 @@
     raw = negs_raw[...].astype(F32)
     unit_neg = raw * lax.rsqrt(jnp.sum(raw * raw, axis=1, keepdims=True))
     neg[pz] = unit_neg.astype(BF16).reshape(neg.shape[1:])
-    lpb[pz] = lp_ref[...]
+    lpb[pz] = jnp.broadcast_to(lp_ref[...].astype(F32), lpb.shape[1:])
     loads[1].wait()
     own_x, inv_x = normalize(ev[...].astype(F32))
     normed_x[...] = own_x
@@ -263,8 +281,7 @@
         ring_arrived(way, s).wait_recv()
         if s + 1 < (ups, dns)[way]:
             ring(way, s + 1).start()
-        for d in range(1, nx):
-            cross(way, s, d).start()
+        cross(way, s, 0).start()
 
     served = [0]
 
@@ -315,7 +332,7 @@
     serve_next()
 
     users = lens_ref.shape[1]
-    lens8 = lens_ref[...].astype(BF16)
+    lens8 = jnp.broadcast_to(lens_ref[...].astype(F32), (8, users)).astype(BF16)
     ri = lax.broadcasted_iota(jnp.int32, (users, users), 0)
     ci = lax.broadcasted_iota(jnp.int32, (users, users), 1)
     before_cols = (ri < ci).astype(F32).astype(BF16)
@@ -344,6 +361,12 @@
     project(0, 3, vb.at[0])
     serve_next(max(ups - 5, 0))
 
+    for way in (0, 1):
+        for s in range((ups, dns)[way]):
+            cross_arrived(way, s, 0).wait_recv()
+            for k in hops[way]:
+                cross(way, s, k).start()
+
     def head_forward(h, carry):
         cols = pl.ds(pl.multiple_of(h * hw, hw), hw)
         keys = kb[:, :, cols].reshape(3 * rows, hw)
@@ -360,8 +383,8 @@
 
     for way in (0, 1):
         for s in range((ups, dns)[way]):
-            for d in range(1, nx):
-                cross_arrived(way, s, d).wait_recv()
+            for k in hops[way]:
+                cross_arrived(way, s, k).wait_recv()
             sib_copy(way, s).start()
 
     normed_o, inv_o = normalize(mixed[...])
@@ -443,14 +466,27 @@
         left = jnp.concatenate([mine, theirs], axis=1)
         return dot(left, gl2[...].reshape(2 * rows, width))
 
-    def dwx(d):
+    wide = width // 2
+
+    def dwx(side, i):
         return remote(
-            send_a.at[d - 1], recv_x.at[d - 1], dwx_s.at[d - 1], dwx_r.at[d - 1], at_x(d)
+            send_a.at[side, i], recv_x.at[side, i], dwx_s.at[side, i], dwx_r.at[side, i], (dev_a, dev_b)[side]
         )
 
-    for d in range(1, nx):
-        send_a[d - 1] = weight_part(lax.rem(sx + d, nx)).astype(BF16).reshape(send_a.shape[1:])
-        dwx(d).start()
+    def dwx2(side):
+        return remote(
+            send_a2.at[side], recv_x2.at[side], dwx_s.at[side, 2], dwx_r.at[side, 2], (dev_b, dev_a)[side]
+        )
+
+    part = weight_part(lax.rem(sx + 2, nx))
+    for side in (0, 1):
+        send_a[side, 0] = part[:, side * wide : (side + 1) * wide].astype(BF16).reshape(send_a.shape[2:])
+        dwx(side, 0).start()
+    for side, at in ((0, xa), (1, xb)):
+        part = weight_part(at)
+        send_a[side, 1] = part[:, side * wide : (side + 1) * wide].astype(BF16).reshape(send_a.shape[2:])
+        dwx(side, 1).start()
+        part_x[1 - side] = part[:, (1 - side) * wide : (2 - side) * wide].reshape(part_x.shape[1:])
     own_b[...] = weight_part(sx).reshape(own_b.shape)
 
     def head_query(h, carry):
@@ -469,46 +505,73 @@
         gm_hop(0, p).wait_recv()
         gm_hop(1, p).start()
 
-    for p in range(HALVES):
-        halo(3, p).wait_recv()
-    project(4, 1, qb.at[2])
-
     def dwy(d):
         return remote(
             send_b.at[lax.rem(yy + d, ny)], recv_y.at[d - 1], dwy_s.at[d - 1], dwy_r.at[d - 1], at_y(d)
         )
 
-    for d in range(1, nx):
-        dwx(d).wait_recv()
-    summed = own_b[...]
-    for d in range(1, nx):
-        summed = summed + recv_x[d - 1].astype(F32)
-    own_b[...] = summed
-    send_b[...] = summed.astype(BF16)
+    def head_keys(lo, count):
+        def body(h, carry):
+            cols = pl.ds(pl.multiple_of(h * hw, hw), hw)
+            queries = qb[lo : lo + count, :, cols].reshape(count * rows, hw)
+            grads = gm[lo : lo + count, :, cols].reshape(count * rows, hw)
+            s = dot(kb[2, :, cols], queries, NT) * scale
+            sg = jax.nn.sigmoid(s)
+            seen = mask_t[:, lo * rows : (lo + count) * rows]
+            w = (s * sg * seen).astype(BF16)
+            gv = dot(w, grads)
+            gs = (dot(vb[2, :, cols], grads, NT) * seen * (sg * (1.0 + s * (1.0 - sg)))).astype(BF16)
+            gk = dot(gs, queries)
+            if lo == 0:
+                gvals[:, cols] = gv
+                gkeys[:, cols] = gk
+                return carry
+            gv = gv + gvals[:, cols]
+            gk = (gk + gkeys[:, cols]) * scale
+            at = pl.ds(pl.multiple_of(2 * width + h * hw, hw), hw)
+            gpre[:, at] = (gk * slopes[2, :, cols]).astype(BF16)
+            at = pl.ds(pl.multiple_of(3 * width + h * hw, hw), hw)
+            gpre[:, at] = (gv * slopes[3, :, cols]).astype(BF16)
+            return carry
+
+        lax.fori_loop(0, heads, body, 0)
+
+    head_keys(0, 2)
+
+    for side in (0, 1):
+        dwx(side, 0).wait_recv()
+        send_a2[side] = (part_x[side] + recv_x[side, 0].astype(F32)).astype(BF16)
+        dwx2(side).start()
+
+    for p in range(HALVES):
+        halo(3, p).wait_recv()
+    project(4, 1, qb.at[2])
+    for p in range(HALVES):
+        gm_hop(1, p).wait_recv()
+    head_keys(2, 1)
+
+    for side in (0, 1):
+        dwx(side, 1).wait_recv()
+        dwx2(side).wait_recv()
+        half_cols = pl.ds(side * wide, wide)
+        summed = own_b[:, :, half_cols] + recv_x[side, 1].astype(F32) + recv_x2[side].astype(F32)
+        own_b[:, :, half_cols] = summed
+        send_b[:, :, half_cols] = summed.astype(BF16)
     for d in range(1, ny):
         dwy(d).start()
 
-    for p in range(HALVES):
-        gm_hop(1, p).wait_recv()
-
-    def head_keys(h, carry):
-        cols = pl.ds(pl.multiple_of(h * hw, hw), hw)
-        queries = qb[:, :, cols].reshape(3 * rows, hw)
-        grads = gm[:, :, cols].reshape(3 * rows, hw)
-        s = dot(kb[2, :, cols], queries, NT) * scale
-        sg = jax.nn.sigmoid(s)
-        seen = mask_t[...]
-        w = (s * sg * seen).astype(BF16)
-        gv = dot(w, grads)
-        gs = (dot(vb[2, :, cols], grads, NT) * seen * (sg * (1.0 + s * (1.0 - sg)))).astype(BF16)
-        gk = dot(gs, queries) * scale
-        at = pl.ds(pl.multiple_of(2 * width + h * hw, hw), hw)
-        gpre[:, at] = (gk * slopes[2, :, cols]).astype(BF16)
-        at = pl.ds(pl.multiple_of(3 * width + h * hw, hw), hw)
-        gpre[:, at] = (gv * slopes[3, :, cols]).astype(BF16)
+    def x_back(j, carry):
+        cols = pl.ds(pl.multiple_of(j * cb, cb), cb)
+        part = dot(gpre[:, 0:width], win[0, cols, :], NT)
+        for c in range(1, 4):
+            part = part + dot(gpre[:, c * width : (c + 1) * width], win[c, cols, :], NT)
+        gact[:, cols] = part
         return carry
 
-    lax.fori_loop(0, heads, head_keys, 0)
+    lax.fori_loop(0, width // cb, x_back, 0)
+    dout[...] = norm_back(gact[...], normed_x[...], inv_x) + gout[...]
+    out_copy = pltpu.make_async_copy(dout, dev_hbm, load_sem.at[8])
+    out_copy.start()
 
     def dwz(d):
         return remote(
@@ -538,16 +601,6 @@
         @pl.when(lax.rem(pz + d, nz) < reds)
         def _(d=d):
             dwz(d).start()
-
-    def x_back(j, carry):
-        cols = pl.ds(pl.multiple_of(j * cb, cb), cb)
-        part = dot(gpre[:, 0:width], win[0, cols, :], NT)
-        for c in range(1, 4):
-            part = part + dot(gpre[:, c * width : (c + 1) * width], win[c, cols, :], NT)
-        gact[:, cols] = part
-        return carry
-
-    lax.fori_loop(0, width // cb, x_back, 0)
 
     @pl.when(pz < reds)
     def _():
@@ -560,10 +613,6 @@
         for d in range(1, nz):
             fin_copy(d).start()
 
-    dout[...] = norm_back(gact[...], normed_x[...], inv_x) + gout[...]
-    out_copy = pltpu.make_async_copy(dout, dev_hbm, load_sem.at[8])
-    out_copy.start()
-
     for d in range(1, nz):
 
         @pl.when(lax.rem(pz - d + nz, nz) < reds)
@@ -582,15 +631,17 @@
     for way in (0, 1):
         for s in range((ups, dns)[way]):
             ring(way, s).wait_send()
-            for d in range(1, nx):
-                cross(way, s, d).wait_send()
+            for k in (0, *hops[way]):
+                cross(way, s, k).wait_send()
             sib_copy(way, s).wait_send()
     for d in range(1, nz):
         lp_copy(d).wait_send()
     to_sib_g.wait_send()
     to_sib_l.wait_send()
-    for d in range(1, nx):
-        dwx(d).wait_send()
+    for side in (0, 1):
+        dwx(side, 0).wait_send()
+        dwx(side, 1).wait_send()
+        dwx2(side).wait_send()
     for d in range(1, ny):
         dwy(d).wait_send()
     for d in range(1, nz):
@@ -617,8 +668,8 @@
     out_rows = width // (ndp * nx)
     piece_rows = rows // (2 * nx)
     events_all = rows * ndp * nx * nz
-    lens8 = jnp.broadcast_to(lengths.astype(F32)[None, :], (8, users))
-    lp8 = jnp.broadcast_to(log_probs.astype(F32)[None, :], (8, rows))
+    lens = lengths.reshape(1, users)
+    lps = log_probs.reshape(1, rows)
     v = pltpu.VMEM
     dma = pltpu.SemaphoreType.DMA
     scratch = [
@@ -650,8 +701,13 @@
         v((rows, width), F32),
         v((rows, 4 * width), BF16),
         v((rows, width), F32),
-        v((nx - 1, ny, out_rows, width), BF16),
-        v((nx - 1, ny, out_rows, width), BF16),
+        v((rows, width), F32),
+        v((rows, width), F32),
+        v((2, 2, ny, out_rows, width // 2), BF16),
+        v((2, 2, ny, out_rows, width // 2), BF16),
+        v((2, ny, out_rows, width // 2), BF16),
+        v((2, ny, out_rows, width // 2), BF16),
+        v((2, ny, out_rows, width // 2), F32),
         v((ny, out_rows, width), F32),
         v((ny, out_rows, width), BF16),
         v((ny - 1, out_rows, width), BF16),
@@ -666,16 +722,16 @@
         dma((2, HALVES)),
         dma((2, ups)),
         dma((2, ups)),
-        dma((2, ups, nx - 1)),
-        dma((2, ups, nx - 1)),
+        dma((2, ups, 3)),
+        dma((2, ups, 3)),
         dma((2, ups)),
         dma((2, ups)),
         dma((nz - 1,)),
         dma((nz - 1,)),
         dma((2,)),
         dma((2,)),
-        dma((nx - 1,)),
-        dma((nx - 1,)),
+        dma((2, 3)),
+        dma((2, 3)),
         dma((ny - 1,)),
         dma((ny - 1,)),
         dma((nz - 1,)),
@@ -697,7 +753,7 @@
         compiler_params=pltpu.CompilerParams(
             collective_id=0, has_side_effects=True, vmem_limit_bytes=56 * 1024 * 1024
         ),
-    )(lens8, lp8, events, input_weight, output_weight, positives, negatives)
+    )(lens, lps, events, input_weight, output_weight, positives, negatives)
 
 
 def solution(mesh):

time: 117 us -> 115 us (0.983)
    broadcast_in_dim x2 -> x0, local copies, waits for them, and re-layouts: 1.86 us -> none  [the longest x1 1.25 us: shards(): lp8 = jnp.broadcast_to(log_probs.astype(F32)[None, :], (8, rows))]
    reshape x0 -> x1, local copies, waits for them, and re-layouts: none -> 1.27 us  [shards(): lens = lengths.reshape(1, users)]
where the time goes in v2:
time: 115 us
  Pallas kernels  109 us (95%)
  local copies, waits for them, and re-layouts  4.63 us (4%)
    pallas_call x1, Pallas kernels, shards(): pl.pallas_call(functools.partial(kernel, (ny, nx, nz, width, heads, event...  109 us
    unnamed x2, local copies, waits for them, and re-layouts  3.36 us

profile of v2, /device:TPU:6, one launch (start us, length us, event | category | flops | bytes accessed | tf_op | source)
XLA Modules:
  0.0 114.7 jit_solution(12880134210459979673)
XLA Ops:
  0.6 1.3 %reshape.10.lens_ref = s32[1,768]{1,0:T(1,128)} reshape(s32[768]{0:T(1024)} %param.13) | data formatting | bytes 6144 | tf_op jit(solution)/shard_map/reshape | solution.py:671
  1.9 109.4 %shard_map.86 = (f32[128,1024]{1,0:T(8,128)}, f32[16,1024]{1,0:T(8,128)}) custom-call(s32[1,768]{1,0:T(1,128)} %reshape.10.lens_ref, bf16[1,128]{1,0:T(2,128)(2,1)} %bitcast.1, bf16[128,1024]{1,0:T(8,128)(2,1)} %ev_hbm.1, bf16[1024,4096]{1,0:T(8,128)(2,1)} %win_hbm.1, bf16[1024,1024]{1,0:T(8,128)(2,1)} %wout_hbm.1, bf16[128,1024]{1,0:T(8,128)(2,1)} %pos_hbm.1, ...), custom_call_target="tpu_custom_call" | custom-call | tf_op jit(solution)/shard_map/pallas_call | solution.py:744
  111.3 1.9 %copy.11 = f32[128,1024]{1,0:T(8,128)} copy(f32[128,1024]{1,0:T(8,128)} %get-tuple-element.4) | data formatting | bytes 1048576
  113.2 1.5 %copy.12 = f32[16,1024]{1,0:T(8,128)} copy(f32[16,1024]{1,0:T(8,128)} %get-tuple-element.5) | data formatting | bytes 131072

commit v3 on v2

--- a/solution.py
+++ b/solution.py
@@ -96,10 +96,8 @@
     own_b,
     send_b,
     recv_y,
-    own_c,
-    send_c,
-    recv_z,
-    fin,
+    line_a,
+    line_b,
     load_sem,
     halo_s,
     halo_r,
@@ -128,10 +126,8 @@
     hw = width // heads
     rows = EV_DEV
     cb = 256
-    ups, dns = nz // 2, nz - 1 - nz // 2
-    reds = fin.shape[0]
-    tw = fin.shape[2]
-    out_rows = fin.shape[1]
+    inner, outer = line_a.shape[0], line_b.shape[0]
+    out_rows = line_a.shape[1]
     scale = 1.0 / math.sqrt(hw)
 
     dp = lax.axis_index("dp")
@@ -205,62 +201,53 @@
             gm.at[kind, part], gm.at[kind + 1, part], gm_s.at[kind, p], gm_r.at[kind, p], prv
         )
 
-    piece = core * nx + sx
-
-    def shard_at(way, s):
-        return lax.rem(pz - s + nz, nz) if way == 0 else lax.rem(pz + s, nz)
-
-    def ring(way, s):
-        ref = neg.at[shard_at(way, s), piece]
+    colour = lax.rem(sx + 2 * yy, nx)
+    piece = core * nx + colour
+    hops = sorted(range(1, nz), key=lambda d: (min(d, nz - d), d))
+    dev_up = (dp, lax.rem(sx + 1, nx), pz)
+    dev_down = (dp, lax.rem(sx + nx - 1, nx), pz)
+
+    near = nz // 2
+    batches = (pl.ds(1, near), pl.ds(1 + near, nz - 1 - near))
+
+    def ring(i):
+        b = 0 if i < near else 1
         return remote(
-            ref, ref, ring_s.at[way, s], ring_r.at[way, s], at_z(1) if way == 0 else at_z(nz - 1)
+            neg.at[0, piece], neg.at[i + 1, piece], ring_s.at[b], ring_r.at[b], at_z(hops[i])
         )
 
-    def ring_arrived(way, s):
-        ref = neg.at[shard_at(way, s + 1), piece]
-        dev = at_z(1) if way == 0 else at_z(nz - 1)
-        return remote(ref, ref, ring_s.at[way, s], ring_r.at[way, s], dev)
-
-    def cross(way, s, k):
-        to_a = (way == 0) == (k == 0)
-        z = shard_at(way, s + 1)
-        if way == 0 and k == 1:
-            ref = neg.at[z, pl.ds(core * nx + 2 * lax.div(sx, 2), 2)]
-        else:
-            ref = neg.at[z, core * nx + (sx, sx, xb)[k]]
-        return remote(ref, ref, xs_s.at[way, s, k], xs_r.at[way, s, k], dev_a if to_a else dev_b)
-
-    def cross_arrived(way, s, k):
-        z = shard_at(way, s + 1)
-        if way == 0:
-            ref = neg.at[z, core * nx + xa] if k == 0 else neg.at[z, pl.ds(core * nx + 2 * lax.div(xb, 2), 2)]
-        else:
-            ref = neg.at[z, core * nx + (xb, xa, nx - 1 - xa)[k]]
-        to_a = (way == 0) == (k == 0)
-        return remote(ref, ref, xs_s.at[way, s, k], xs_r.at[way, s, k], dev_a if to_a else dev_b)
-
-    hops = ((1,), (1, 2))
-
-    def sib_copy(way, s):
-        ref = neg.at[shard_at(way, s + 1), pl.ds(core * nx, nx)]
-        return remote(ref, ref, sib_s.at[way, s], sib_r.at[way, s], sib)
-
-    def sib_arrived(way, s):
-        ref = neg.at[shard_at(way, s + 1), pl.ds((1 - core) * nx, nx)]
-        return remote(ref, ref, sib_s.at[way, s], sib_r.at[way, s], sib)
-
-    def lp_copy(d):
-        return remote(lpb.at[pz], lpb.at[pz], lp_s.at[d - 1], lp_r.at[d - 1], at_z(d))
-
-    def lp_arrived(d):
-        ref = lpb.at[lax.rem(pz - d + nz, nz)]
-        return remote(ref, ref, lp_s.at[d - 1], lp_r.at[d - 1], at_z(d))
+    def ring_all(b):
+        ref = neg.at[batches[b], piece]
+        return remote(ref, ref, ring_s.at[b], ring_r.at[b], at_z(1))
+
+    def cross(b, k, slot=None):
+        ref = neg.at[batches[b], piece if slot is None else slot]
+        dev = (dev_up, dev_down, at_y((1, ny - 1)[b]))[k]
+        return remote(ref, ref, xs_s.at[b, k], xs_r.at[b, k], dev)
+
+    def cross_arrived(b, k):
+        return cross(b, k, core * nx + lax.rem(colour + (3, 1, 2)[k], nx))
+
+    def sib_copy(b):
+        ref = neg.at[batches[b], pl.ds(core * nx, nx)]
+        return remote(ref, ref, sib_s.at[b], sib_r.at[b], sib)
+
+    def sib_arrived(b):
+        ref = neg.at[batches[b], pl.ds((1 - core) * nx, nx)]
+        return remote(ref, ref, sib_s.at[b], sib_r.at[b], sib)
+
+    def lp_copy(i):
+        return remote(lpb.at[0], lpb.at[i + 1], lp_s.at[0], lp_r.at[0], at_z(hops[i]))
+
+    def lp_all():
+        ref = lpb.at[pl.ds(1, nz - 1)]
+        return remote(ref, ref, lp_s.at[0], lp_r.at[0], at_z(1))
 
     loads[0].wait()
     raw = negs_raw[...].astype(F32)
     unit_neg = raw * lax.rsqrt(jnp.sum(raw * raw, axis=1, keepdims=True))
-    neg[pz] = unit_neg.astype(BF16).reshape(neg.shape[1:])
-    lpb[pz] = jnp.broadcast_to(lp_ref[...].astype(F32), lpb.shape[1:])
+    neg[0] = unit_neg.astype(BF16).reshape(neg.shape[1:])
+    lpb[0] = jnp.broadcast_to(lp_ref[...].astype(F32), lpb.shape[1:])
     loads[1].wait()
     own_x, inv_x = normalize(ev[...].astype(F32))
     normed_x[...] = own_x
@@ -271,27 +258,16 @@
     for p in range(HALVES):
         halo(0, p).start()
         halo(1, p).start()
-    ring(0, 0).start()
-    if dns:
-        ring(1, 0).start()
-    for d in range(1, nz):
-        lp_copy(d).start()
-
-    def serve(way, s):
-        ring_arrived(way, s).wait_recv()
-        if s + 1 < (ups, dns)[way]:
-            ring(way, s + 1).start()
-        cross(way, s, 0).start()
-
-    served = [0]
-
-    def serve_next(count=1):
-        for _ in range(count):
-            s = served[0]
-            for way in (0, 1):
-                if s < (ups, dns)[way]:
-                    serve(way, s)
-            served[0] = s + 1
+
+    def serve(b):
+        ring_all(b).wait_recv()
+        for k in range(3):
+            cross(b, k).start()
+
+    def pass_on(b):
+        for k in range(3):
+            cross_arrived(b, k).wait_recv()
+        sib_copy(b).start()
 
     def project_own(chunk, dst):
         def body(j, carry):
@@ -323,16 +299,20 @@
         halo(2, p).start()
         halo(1, p).wait_recv()
         halo(3, p).start()
-    serve_next()
+    for i in range(nz - 1):
+        ring(i).start()
+    for i in range(nz - 1):
+        lp_copy(i).start()
 
     loads[4].wait()
     project_own(1, qb.at[0])
     loads[5].wait()
     project_own(0, upd)
-    serve_next()
-
-    users = lens_ref.shape[1]
-    lens8 = jnp.broadcast_to(lens_ref[...].astype(F32), (8, users)).astype(BF16)
+
+    lens_rows, lens_cols = lens_ref.shape
+    users = lens_rows * lens_cols
+    lens_line = jnp.concatenate([lens_ref[k : k + 1, :] for k in range(lens_rows)], axis=1)
+    lens8 = jnp.broadcast_to(lens_line.astype(F32), (8, users)).astype(BF16)
     ri = lax.broadcasted_iota(jnp.int32, (users, users), 0)
     ci = lax.broadcasted_iota(jnp.int32, (users, users), 1)
     before_cols = (ri < ci).astype(F32).astype(BF16)
@@ -348,24 +328,15 @@
     row_first = jnp.max(jnp.where(starts_col <= row_pos, starts_col, 0.0), axis=0, keepdims=True)
     row_first = jnp.where(row_pos < events_all, row_first, float(2 * events_all))
     mask_t[...] = jnp.where((own_pos >= row_first) & (own_pos <= row_pos), 1.0 / EV_DEV, 0.0)
-    serve_next()
 
     project(1, 2, kb.at[1])
     project(1, 3, vb.at[1])
-    serve_next()
     project(3, 1, qb.at[1])
-    serve_next()
     for p in range(HALVES):
         halo(2, p).wait_recv()
+    serve(0)
     project(0, 2, kb.at[0])
     project(0, 3, vb.at[0])
-    serve_next(max(ups - 5, 0))
-
-    for way in (0, 1):
-        for s in range((ups, dns)[way]):
-            cross_arrived(way, s, 0).wait_recv()
-            for k in hops[way]:
-                cross(way, s, k).start()
 
     def head_forward(h, carry):
         cols = pl.ds(pl.multiple_of(h * hw, hw), hw)
@@ -381,11 +352,7 @@
 
     lax.fori_loop(0, heads, head_forward, 0)
 
-    for way in (0, 1):
-        for s in range((ups, dns)[way]):
-            for k in hops[way]:
-                cross_arrived(way, s, k).wait_recv()
-            sib_copy(way, s).start()
+    serve(1)
 
     normed_o, inv_o = normalize(mixed[...])
     mixed[...] = normed_o
@@ -399,6 +366,8 @@
     unit[...] = unit_out
     unit_low = unit_out.astype(BF16)
 
+    pass_on(0)
+
     per_y = width // ny
     for j in range(ny):
         turned = gated[:, j * per_y : (j + 1) * per_y].T.astype(BF16)
@@ -414,12 +383,8 @@
     pos_unit = pos_rows * lax.rsqrt(jnp.sum(pos_rows * pos_rows, axis=1, keepdims=True))
     pos_exp = jnp.exp(jnp.sum(unit_out * pos_unit, axis=1, keepdims=True) / sharpness_divisor)
 
-    for d in range(1, nz):
-        lp_arrived(d).wait_recv()
-    for way in (0, 1):
-        for s in range((ups, dns)[way]):
-            sib_arrived(way, s).wait_recv()
-
+    pass_on(1)
+    lp_all().wait_recv()
     def logits(z, exp_total):
         negs = neg[z].reshape(rows, width)
         lg = dot(unit_low, negs, NT) * (1.0 / sharpness_divisor) - lpb[z, 0:1, :]
@@ -427,7 +392,10 @@
         ebuf[:, pl.ds(pl.multiple_of(z * rows, rows), rows)] = e.astype(BF16)
         return exp_total + jnp.sum(e, axis=1, keepdims=True)
 
-    exp_total = lax.fori_loop(0, nz, logits, jnp.zeros((rows, 1), F32))
+    exp_total = logits(0, jnp.zeros((rows, 1), F32))
+    for b, (lo, hi) in enumerate(((1, 1 + near), (1 + near, nz))):
+        sib_arrived(b).wait_recv()
+        exp_total = lax.fori_loop(lo, hi, logits, exp_total)
     denominator = pos_exp + exp_total
     mixed_negs = dot(ebuf[...], neg[...].reshape(nz * rows, width))
     unit_out = unit[...]
@@ -507,8 +475,11 @@
 
     def dwy(d):
         return remote(
-            send_b.at[lax.rem(yy + d, ny)], recv_y.at[d - 1], dwy_s.at[d - 1], dwy_r.at[d - 1], at_y(d)
+            send_b.at[lax.rem(yy + d, ny)], recv_y.at[d - 1], dwy_s.at[0], dwy_r.at[0], at_y(d)
         )
+
+    def dwy_all():
+        return remote(recv_y, recv_y, dwy_s.at[0], dwy_r.at[0], at_y(1))
 
     def head_keys(lo, count):
         def body(h, carry):
@@ -573,54 +544,33 @@
     out_copy = pltpu.make_async_copy(dout, dev_hbm, load_sem.at[8])
     out_copy.start()
 
-    def dwz(d):
-        return remote(
-            send_c.at[lax.rem(pz + d, nz)], recv_z.at[d - 1], dwz_s.at[d - 1], dwz_r.at[d - 1], at_z(d)
-        )
-
-    def dwz_arrived(d):
-        return remote(send_c.at[0], recv_z.at[d - 1], dwz_s.at[d - 1], dwz_r.at[d - 1], at_z(d))
-
-    def fin_copy(d):
-        return remote(fin.at[pz], fin.at[pz], fin_s.at[d - 1], fin_r.at[d - 1], at_z(d))
-
-    def fin_arrived(d):
-        ref = fin.at[lax.rem(pz - d + nz, nz)]
-        return remote(ref, ref, fin_s.at[d - 1], fin_r.at[d - 1], at_z(d))
-
-    for d in range(1, ny):
-        dwy(d).wait_recv()
+    row_a, row_b = lax.rem(pz, inner), lax.div(pz, inner)
+
+    def line(which, d, source=False):
+        count = (inner, outer)[which]
+        spot = (row_a, row_b)[which]
+        there = lax.rem(spot + (count - d if source else d), count)
+        to = lax.rem(spot + d, count)
+        buf = (line_a, line_b)[which]
+        ref = buf.at[there if source else spot]
+        dev = (dp, sx, row_b * inner + to) if which == 0 else (dp, sx, to * inner + row_a)
+        return remote(ref, ref, (dwz_s, fin_s)[which].at[d - 1], (dwz_r, fin_r)[which].at[d - 1], dev)
+
+    dwy_all().wait_recv()
     summed = own_b[yy]
     for d in range(1, ny):
         summed = summed + recv_y[d - 1].astype(F32)
-    for t in range(reds):
-        own_c[t] = summed[:, t * tw : (t + 1) * tw]
-        send_c[t] = summed[:, t * tw : (t + 1) * tw].astype(BF16)
-    for d in range(1, nz):
-
-        @pl.when(lax.rem(pz + d, nz) < reds)
-        def _(d=d):
-            dwz(d).start()
-
-    @pl.when(pz < reds)
-    def _():
-        for d in range(1, nz):
-            dwz_arrived(d).wait_recv()
-        done = own_c[pz]
-        for d in range(1, nz):
-            done = done + recv_z[d - 1].astype(F32)
-        fin[pz] = done
-        for d in range(1, nz):
-            fin_copy(d).start()
-
-    for d in range(1, nz):
-
-        @pl.when(lax.rem(pz - d + nz, nz) < reds)
-        def _(d=d):
-            fin_arrived(d).wait_recv()
-
-    for t in range(reds):
-        dw_ref[:, t * tw : (t + 1) * tw] = fin[t]
+    for which in (0, 1):
+        buf, count = ((line_a, inner), (line_b, outer))[which]
+        buf[(row_a, row_b)[which]] = summed.astype(BF16)
+        for d in range(1, count):
+            line(which, d).start()
+        for d in range(1, count):
+            line(which, d, True).wait_recv()
+        summed = buf[0].astype(F32)
+        for k in range(1, count):
+            summed = summed + buf[k].astype(F32)
+    dw_ref[...] = summed
     out_copy.wait()
 
     for p in range(HALVES):
@@ -628,32 +578,27 @@
             halo(kind, p).wait_send()
         for kind in range(2):
             gm_hop(kind, p).wait_send()
-    for way in (0, 1):
-        for s in range((ups, dns)[way]):
-            ring(way, s).wait_send()
-            for k in (0, *hops[way]):
-                cross(way, s, k).wait_send()
-            sib_copy(way, s).wait_send()
-    for d in range(1, nz):
-        lp_copy(d).wait_send()
+    for b in (0, 1):
+        ring_all(b).wait_send()
+        for k in range(3):
+            cross(b, k).wait_send()
+        sib_copy(b).wait_send()
+    lp_all().wait_send()
     to_sib_g.wait_send()
     to_sib_l.wait_send()
     for side in (0, 1):
         dwx(side, 0).wait_send()
         dwx(side, 1).wait_send()
         dwx2(side).wait_send()
-    for d in range(1, ny):
-        dwy(d).wait_send()
-    for d in range(1, nz):
-
-        @pl.when(lax.rem(pz + d, nz) < reds)
-        def _(d=d):
-            dwz(d).wait_send()
-
-    @pl.when(pz < reds)
-    def _():
-        for d in range(1, nz):
-            fin_copy(d).wait_send()
+    dwy_all().wait_send()
+    for which in (0, 1):
+        for d in range(1, (inner, outer)[which]):
+            line(which, d).wait_send()
+
+
+def hand_over(a_ref, b_ref, out_a, out_b):
+    out_a[...] = a_ref[...]
+    out_b[...] = b_ref[...]
 
 
 def shards(mesh_sizes, events, input_weight, output_weight, positives, negatives, log_probs, lengths):
@@ -662,13 +607,12 @@
     rows, width = events.shape
     heads = HEADS
     users = lengths.shape[0]
-    ups = nz // 2
-    reds = 8 if nz >= 8 else 2
-    tw = width // reds
+    outer = 3 if nz % 3 == 0 else 1
+    inner = nz // outer
     out_rows = width // (ndp * nx)
     piece_rows = rows // (2 * nx)
     events_all = rows * ndp * nx * nz
-    lens = lengths.reshape(1, users)
+    lens = lengths.reshape(users // rows, rows)
     lps = log_probs.reshape(1, rows)
     v = pltpu.VMEM
     dma = pltpu.SemaphoreType.DMA
@@ -711,37 +655,35 @@
         v((ny, out_rows, width), F32),
         v((ny, out_rows, width), BF16),
         v((ny - 1, out_rows, width), BF16),
-        v((reds, out_rows, tw), F32),
-        v((reds, out_rows, tw), BF16),
-        v((nz - 1, out_rows, tw), BF16),
-        v((reds, out_rows, tw), F32),
+        v((inner, out_rows, width), BF16),
+        v((outer, out_rows, width), BF16),
         dma((9,)),
         dma((4, HALVES)),
         dma((4, HALVES)),
         dma((2, HALVES)),
         dma((2, HALVES)),
-        dma((2, ups)),
-        dma((2, ups)),
-        dma((2, ups, 3)),
-        dma((2, ups, 3)),
-        dma((2, ups)),
-        dma((2, ups)),
-        dma((nz - 1,)),
-        dma((nz - 1,)),
         dma((2,)),
         dma((2,)),
         dma((2, 3)),
         dma((2, 3)),
-        dma((ny - 1,)),
-        dma((ny - 1,)),
-        dma((nz - 1,)),
-        dma((nz - 1,)),
-        dma((nz - 1,)),
-        dma((nz - 1,)),
+        dma((2,)),
+        dma((2,)),
+        dma((1,)),
+        dma((1,)),
+        dma((2,)),
+        dma((2,)),
+        dma((2, 3)),
+        dma((2, 3)),
+        dma((1,)),
+        dma((1,)),
+        dma((inner,)),
+        dma((inner,)),
+        dma((outer,)),
+        dma((outer,)),
     ]
     hbm = pl.BlockSpec(memory_space=pl.ANY)
     vmem = pl.BlockSpec(memory_space=pltpu.VMEM)
-    return pl.pallas_call(
+    results = pl.pallas_call(
         functools.partial(kernel, (ny, nx, nz, width, heads, events_all)),
         out_shape=(
             jax.ShapeDtypeStruct((rows, width), F32),
@@ -754,6 +696,12 @@
             collective_id=0, has_side_effects=True, vmem_limit_bytes=56 * 1024 * 1024
         ),
     )(lens, lps, events, input_weight, output_weight, positives, negatives)
+    return pl.pallas_call(
+        hand_over,
+        out_shape=tuple(jax.ShapeDtypeStruct(r.shape, r.dtype) for r in results),
+        in_specs=[vmem, vmem],
+        out_specs=(vmem, vmem),
+    )(*results)
 
 
 def solution(mesh):

time: 115 us -> 104 us (0.904)
  Pallas kernels: 109 us -> 103 us
  local copies, waits for them, and re-layouts: 4.63 us -> 0 us
    pallas_call x1, Pallas kernels: 109 us -> 101 us  [shards(): pl.pallas_call(functools.partial(kernel, (ny, nx, nz, width, heads, event...]
    unnamed x2 -> x0, local copies, waits for them, and re-layouts: 3.36 us -> none
    pallas_call x0 -> x1, Pallas kernels: none -> 1.88 us  [shards(): pl.pallas_call(hand_over, out_shape=tuple((jax.ShapeDtypeStruct(r.shape,...]
    reshape x1 -> x0, local copies, waits for them, and re-layouts: 1.27 us -> none  [shards(): lens = lengths.reshape(1, users)]
where the time goes in v3:
time: 104 us
  Pallas kernels  103 us (99%)
    pallas_call x1, Pallas kernels, shards(): pl.pallas_call(functools.partial(kernel, (ny, nx, nz, width, heads, event...  101 us

profile of v3, /device:TPU:6, one launch (start us, length us, event | category | flops | bytes accessed | tf_op | source)
XLA Modules:
  0.0 103.9 jit_solution(4595273374293062164)
XLA Ops:
  0.6 101.4 %shard_map.86 = (f32[128,1024]{1,0:T(8,128)}, f32[16,1024]{1,0:T(8,128)}) custom-call(s32[6,128]{1,0:T(8,128)} %bitcast.2, bf16[1,128]{1,0:T(2,128)(2,1)} %bitcast.3, bf16[128,1024]{1,0:T(8,128)(2,1)} %ev_hbm.1, bf16[1024,4096]{1,0:T(8,128)(2,1)} %win_hbm.1, bf16[1024,1024]{1,0:T(8,128)(2,1)} %wout_hbm.1, bf16[128,1024]{1,0:T(8,128)(2,1)} %pos_hbm.1, ...), custom_call_target="tpu_custom_call" | custom-call | tf_op jit(solution)/shard_map/pallas_call | solution.py:686
  102.0 1.9 %shard_map.87 = (f32[128,1024]{1,0:T(8,128)}, f32[16,1024]{1,0:T(8,128)}) custom-call(f32[128,1024]{1,0:T(8,128)} %get-tuple-element.4.a_ref, f32[16,1024]{1,0:T(8,128)} %get-tuple-element.5.b_ref), custom_call_target="tpu_custom_call" | custom-call | tf_op jit(solution)/shard_map/pallas_call | solution.py:699

commit v4 on v3

--- a/solution.py
+++ b/solution.py
@@ -258,6 +258,8 @@
     for p in range(HALVES):
         halo(0, p).start()
         halo(1, p).start()
+    for i in range(near):
+        ring(i).start()
 
     def serve(b):
         ring_all(b).wait_recv()
@@ -299,7 +301,7 @@
         halo(2, p).start()
         halo(1, p).wait_recv()
         halo(3, p).start()
-    for i in range(nz - 1):
+    for i in range(near, nz - 1):
         ring(i).start()
     for i in range(nz - 1):
         lp_copy(i).start()
@@ -332,9 +334,9 @@
     project(1, 2, kb.at[1])
     project(1, 3, vb.at[1])
     project(3, 1, qb.at[1])
+    serve(0)
     for p in range(HALVES):
         halo(2, p).wait_recv()
-    serve(0)
     project(0, 2, kb.at[0])
     project(0, 3, vb.at[0])
 
@@ -350,9 +352,11 @@
         mixed[:, cols] = dot(w, values)
         return carry
 
-    lax.fori_loop(0, heads, head_forward, 0)
-
+    lax.fori_loop(0, heads // 2, head_forward, 0)
+    pass_on(0)
     serve(1)
+    lax.fori_loop(heads // 2, heads, head_forward, 0)
+
 
     normed_o, inv_o = normalize(mixed[...])
     mixed[...] = normed_o
@@ -366,7 +370,6 @@
     unit[...] = unit_out
     unit_low = unit_out.astype(BF16)
 
-    pass_on(0)
 
     per_y = width // ny
     for j in range(ny):

time: 104 us -> 102 us (0.981)
  Pallas kernels: 103 us -> 101 us
    pallas_call x1, Pallas kernels: 101 us -> 98.9 us  [shards(): pl.pallas_call(functools.partial(kernel, (ny, nx, nz, width, heads, event...]
where the time goes in v4:
time: 102 us; the launch traced here: 101 us
  Pallas kernels  101 us (99%)
    pallas_call x1, Pallas kernels, shards(): pl.pallas_call(functools.partial(kernel, (ny, nx, nz, width, heads, event...  98.9 us

profile of v4, /device:TPU:6, one launch (start us, length us, event | category | flops | bytes accessed | tf_op | source)
XLA Modules:
  0.0 101.4 jit_solution(3514178222325022195)
XLA Ops:
  0.6 98.9 %shard_map.86 = (f32[128,1024]{1,0:T(8,128)}, f32[16,1024]{1,0:T(8,128)}) custom-call(s32[6,128]{1,0:T(8,128)} %bitcast.2, bf16[1,128]{1,0:T(2,128)(2,1)} %bitcast.3, bf16[128,1024]{1,0:T(8,128)(2,1)} %ev_hbm.1, bf16[1024,4096]{1,0:T(8,128)(2,1)} %win_hbm.1, bf16[1024,1024]{1,0:T(8,128)(2,1)} %wout_hbm.1, bf16[128,1024]{1,0:T(8,128)(2,1)} %pos_hbm.1, ...), custom_call_target="tpu_custom_call" | custom-call | tf_op jit(solution)/shard_map/pallas_call | solution.py:689
  99.5 1.9 %shard_map.87 = (f32[128,1024]{1,0:T(8,128)}, f32[16,1024]{1,0:T(8,128)}) custom-call(f32[128,1024]{1,0:T(8,128)} %get-tuple-element.4.a_ref, f32[16,1024]{1,0:T(8,128)} %get-tuple-element.5.b_ref), custom_call_target="tpu_custom_call" | custom-call | tf_op jit(solution)/shard_map/pallas_call | solution.py:702

commit v5 on v4

--- a/solution.py
+++ b/solution.py
@@ -352,10 +352,10 @@
         mixed[:, cols] = dot(w, values)
         return carry
 
-    lax.fori_loop(0, heads // 2, head_forward, 0)
+    lax.fori_loop(0, heads // 2, head_forward, 0, unroll=2)
     pass_on(0)
     serve(1)
-    lax.fori_loop(heads // 2, heads, head_forward, 0)
+    lax.fori_loop(heads // 2, heads, head_forward, 0, unroll=2)
 
 
     normed_o, inv_o = normalize(mixed[...])
@@ -421,13 +421,6 @@
         return carry
 
     lax.fori_loop(0, width // cb, gate_back, 0)
-    grad_gated = gact[...]
-    normed_o = mixed[...]
-    gpre[:, 0:width] = (grad_gated * normed_o * slopes[0]).astype(BF16)
-    gm[0] = norm_back(grad_gated * upd[...].astype(F32), normed_o, inv_o).astype(BF16)
-    for p in range(HALVES):
-        gm_hop(0, p).start()
-
     to_sib_g.wait_recv()
     to_sib_l.wait_recv()
 
@@ -458,6 +451,13 @@
         send_a[side, 1] = part[:, side * wide : (side + 1) * wide].astype(BF16).reshape(send_a.shape[2:])
         dwx(side, 1).start()
         part_x[1 - side] = part[:, (1 - side) * wide : (2 - side) * wide].reshape(part_x.shape[1:])
+    grad_gated = gact[...]
+    normed_o = mixed[...]
+    gpre[:, 0:width] = (grad_gated * normed_o * slopes[0]).astype(BF16)
+    gm[0] = norm_back(grad_gated * upd[...].astype(F32), normed_o, inv_o).astype(BF16)
+    for p in range(HALVES):
+        gm_hop(0, p).start()
+
     own_b[...] = weight_part(sx).reshape(own_b.shape)
 
     def head_query(h, carry):
@@ -470,7 +470,7 @@
         gpre[:, at] = (gq * slopes[1, :, cols]).astype(BF16)
         return carry
 
-    lax.fori_loop(0, heads, head_query, 0)
+    lax.fori_loop(0, heads, head_query, 0, unroll=2)
 
     for p in range(HALVES):
         gm_hop(0, p).wait_recv()
@@ -508,7 +508,7 @@
             gpre[:, at] = (gv * slopes[3, :, cols]).astype(BF16)
             return carry
 
-        lax.fori_loop(0, heads, body, 0)
+        lax.fori_loop(0, heads, body, 0, unroll=2)
 
     head_keys(0, 2)
 

time: 102 us -> 103 us (level); the launches traced: 101 us -> 101 us
  no operation moved by 1% of the time
where the time goes in v5:
time: 103 us; the launch traced here: 101 us
  Pallas kernels  101 us (98%)
    pallas_call x1, Pallas kernels, shards(): pl.pallas_call(functools.partial(kernel, (ny, nx, nz, width, heads, event...  98.9 us

profile of v5, /device:TPU:6, one launch (start us, length us, event | category | flops | bytes accessed | tf_op | source)
XLA Modules:
  0.0 101.4 jit_solution(228444102553363877)
XLA Ops:
  0.6 98.9 %shard_map.86 = (f32[128,1024]{1,0:T(8,128)}, f32[16,1024]{1,0:T(8,128)}) custom-call(s32[6,128]{1,0:T(8,128)} %bitcast.2, bf16[1,128]{1,0:T(2,128)(2,1)} %bitcast.3, bf16[128,1024]{1,0:T(8,128)(2,1)} %ev_hbm.1, bf16[1024,4096]{1,0:T(8,128)(2,1)} %win_hbm.1, bf16[1024,1024]{1,0:T(8,128)(2,1)} %wout_hbm.1, bf16[128,1024]{1,0:T(8,128)(2,1)} %pos_hbm.1, ...), custom_call_target="tpu_custom_call" | custom-call | tf_op jit(solution)/shard_map/pallas_call | solution.py:689
  99.5 1.9 %shard_map.87 = (f32[128,1024]{1,0:T(8,128)}, f32[16,1024]{1,0:T(8,128)}) custom-call(f32[128,1024]{1,0:T(8,128)} %get-tuple-element.4.a_ref, f32[16,1024]{1,0:T(8,128)} %get-tuple-element.5.b_ref), custom_call_target="tpu_custom_call" | custom-call | tf_op jit(solution)/shard_map/pallas_call | solution.py:702
